TPU v7x, 512 devices: a whole 4x4x16 slice. The times are simulated.
512 devices in a mesh: tm: 16 (over z_lo, core), space: 32 (over z_hi, x, y).
Axes of the slice: x: 4, y: 4, z: 16 (z_hi: 2, z_lo: 8; z = z_hi * 8 + z_lo), core: 2. Of those that a mesh axis runs over, the one named last changes fastest.
Arguments:
- starts: float32 [16, 512, 16, 512], P('tm', 'space'), may hold values from -6 to 6
- zone_map: int32 [512, 16, 512], P('space'), may hold values from 0 to 15
- zone_velocity: int32 [16], replicated, may hold values from 0 to 15, each once
- conductivity: float32 [16], replicated, may hold values from 0.002 to 0.015
- x_velocity: float32 [16], replicated, may hold values from -0.7 to 0.7
- cross_velocity: float32 [2, 16], replicated, may hold values from -0.1 to 0.1
- coarse_kernel: float32 [3, 3, 3], replicated, may hold values from 0 to 0.2
Outputs:
- corrected: float32 [16, 512, 16, 512], P('tm', 'space')
Inputs may be any that keep to these rules, and one draw needn't show every extreme that they name: `zone_velocity`: each of the 16 velocity sets is named by exactly one zone.
All inputs are finite; a program needn't handle non-finite values.
Results may differ from a plain program's by a relative error of at most 0.00002.
Values sent between devices are 32-bit elements; how exact they have to be, the bound alone decides.
A program may use at most 64 MiB of HBM per device.

v0:
```python
import jax
import jax.numpy as jnp
from jax import lax
from jax.sharding import PartitionSpec as P

FINE = 16
ZONES = 16


def extended_2(shard, sides, width):
    for axis, dim in sides:
        count, length = (lax.axis_size(axis), shard.shape[dim])
        up = [(i, (i + 1) % count) for i in range(count - 1)]
        down = [(j, i) for i, j in up]
        last = lax.slice_in_dim(shard, length - width, length, axis=dim)
        leading = lax.slice_in_dim(shard, 0, width, axis=dim)
        before = lax.ppermute(last, axis, up)
        after = lax.ppermute(leading, axis, down)
        shard = jnp.concatenate([before, shard, after], axis=dim)
    return shard


def passed_along(shard, axis, by):
    count = lax.axis_size(axis)
    pairs = [(i, i + by) for i in range(count) if 0 <= i + by < count]
    return lax.ppermute(shard, axis, pairs)


def coefficients(zone_map, zone_velocity, conductivity, x_velocity, cross_velocity):
    chosen = (
        zone_velocity[:, None] == jnp.arange(x_velocity.shape[0], dtype=jnp.int32)[None, :]
    ).astype(jnp.float32)
    lookup = jnp.stack(
        [
            conductivity,
            jnp.sum(chosen * x_velocity[None, :], axis=1),
            jnp.sum(chosen * cross_velocity[1][None, :], axis=1),
            jnp.sum(chosen * cross_velocity[0][None, :], axis=1),
        ]
    )
    coef_stack = jnp.zeros((4,) + zone_map.shape, jnp.float32)
    for zone_index in range(ZONES):
        coef_stack = coef_stack + jnp.where(
            zone_map[None] == zone_index,
            lookup[:, zone_index][:, None, None, None],
            jnp.float32(0.0),
        )
    return coef_stack


def upwind(courant, values, lower, upper):
    return jnp.maximum(courant, 0.0) * (values - lower) + jnp.minimum(courant, 0.0) * (
        upper - values
    )


def advance(values, coef_stack):
    padded = jnp.pad(values, 1)
    x_lower = padded[:-2, 1:-1, 1:-1]
    x_upper = padded[2:, 1:-1, 1:-1]
    z_lower = padded[1:-1, :-2, 1:-1]
    z_upper = padded[1:-1, 2:, 1:-1]
    y_lower = padded[1:-1, 1:-1, :-2]
    y_upper = padded[1:-1, 1:-1, 2:]
    transport = upwind(coef_stack[1], values, x_lower, x_upper)
    transport = transport + upwind(coef_stack[2], values, z_lower, z_upper)
    transport = transport + upwind(coef_stack[3], values, y_lower, y_upper)
    laplace = x_lower + x_upper + z_lower + z_upper + y_lower + y_upper - 6.0 * values
    return values - transport + coef_stack[0] * laplace


def coarse(values, kernel):
    extended = extended_2(values, (("space", 0),), 1)
    padded = jnp.pad(extended, ((0, 0), (1, 1), (1, 1)))
    total = jnp.zeros_like(values)
    for x_offset in range(3):
        for z_offset in range(3):
            for y_offset in range(3):
                total = (
                    total
                    + kernel[x_offset, z_offset, y_offset]
                    * padded[
                        x_offset : x_offset + values.shape[0],
                        z_offset : z_offset + values.shape[1],
                        y_offset : y_offset + values.shape[2],
                    ]
                )
    return total


def shards(
    starts, zone_map, zone_velocity, conductivity, x_velocity, cross_velocity, coarse_kernel
):
    initial = starts[0]
    row_count = initial.shape[0]
    slice_index = lax.axis_index("tm")
    coef_stack = coefficients(zone_map, zone_velocity, conductivity, x_velocity, cross_velocity)
    rim_depth = 8
    wide_coefs = extended_2(coef_stack, (("space", 1),), rim_depth)
    values = initial
    for block_index in range(FINE // rim_depth):
        extended = extended_2(values, (("space", 0),), rim_depth)
        extended = lax.fori_loop(
            0, rim_depth, lambda turn_index, current: advance(current, wide_coefs), extended
        )
        values = extended[rim_depth : rim_depth + row_count]
    fine_end = values
    jump_term = fine_end - coarse(initial, coarse_kernel)

    def relay_round(turn_index, carried):
        corrected_here = jnp.where(
            slice_index == 0, fine_end, coarse(carried, coarse_kernel) + jump_term
        )
        return passed_along(corrected_here, "tm", 1)

    carried = lax.fori_loop(0, lax.axis_size("tm") - 1, relay_round, jnp.zeros_like(fine_end))
    corrected = jnp.where(slice_index == 0, fine_end, coarse(carried, coarse_kernel) + jump_term)
    return corrected[None]


def solution(mesh):
    in_specs = (P("tm", "space", None, None), P("space", None, None), P(), P(), P(), P(), P())
    out_specs = P("tm", "space", None, None)
    return jax.shard_map(shards, mesh=mesh, in_specs=in_specs, out_specs=out_specs, check_vma=False)
```

profile of v0, /device:TPU:62, one launch (start us, length us, event | category | flops | bytes accessed | tf_op | source)
XLA Modules:
  0.0 1099.2 jit_solution(899603242390230536)
XLA Ops:
  9.9 14.4 %collective-permute-start.5 = (f32[4,8,16,512]{3,2,1,0:T(8,128)}, f32[4,8,16,512]{3,2,1,0:T(8,128)}, u32[]{:S(2)}, u32[]{:S(2)}) collective-permute-start(f32[4,8,16,512]{3,2,1,0:T(8,128)} %get-tuple-element.241), channel_id=1, source_target_pairs={{0,1},{1,2},{2,3},{3,4},{4,5},{5,6},{6,7},{7,8},{8,9},{9,10},{10,1... | collective-permute-start | bytes 3145736 | tf_op jit(solution)/shard_map/ppermute | solution.py:17
  26.3 16.9 %collective-permute-start.3 = (f32[8,16,512]{2,1,0:T(8,128)S(1)}, f32[8,16,512]{2,1,0:T(8,128)S(1)}, u32[]{:S(2)}, u32[]{:S(2)}) collective-permute-start(f32[8,16,512]{2,1,0:T(8,128)S(1)} %get-tuple-element.263), channel_id=1, source_target_pairs={{0,1},{1,2},{2,3},{3,4},{4,5},{5,6},{6,7},{7,8},{8,9},{9,10},{10,1... | collective-permute-start | bytes 786440 | tf_op jit(solution)/shard_map/ppermute | solution.py:17
  48.5 101.7 %collective-permute-done.3 = f32[8,16,512]{2,1,0:T(8,128)S(1)} collective-permute-done((f32[8,16,512]{2,1,0:T(8,128)S(1)}, f32[8,16,512]{2,1,0:T(8,128)S(1)}, u32[]{:S(2)}, u32[]{:S(2)}) %collective-permute-start.3) | collective-permute-done | bytes 262176 | tf_op jit(solution)/shard_map/ppermute | solution.py:17
  150.1 17.3 %collective-permute-start.9 = (f32[1,16,512]{2,1,0:T(8,128)S(1)}, f32[1,16,512]{2,1,0:T(8,128)S(1)}, u32[]{:S(2)}, u32[]{:S(2)}) collective-permute-start(f32[1,16,512]{2,1,0:T(8,128)S(1)} %get-tuple-element.265), channel_id=1, source_target_pairs={{0,1},{1,2},{2,3},{3,4},{4,5},{5,6},{6,7},{7,8},{8,9},{9,10},{10,1... | collective-permute-start | bytes 98312 | tf_op jit(solution)/shard_map/ppermute | solution.py:17
  167.6 4.2 pad_maximum_fusion.2
  171.8 27.9 %while.36 = (s32[]{:T(128)}, f32[32,16,512]{2,1,0:T(8,128)S(1)}, f32[4,32,16,512]{3,2,1,0:T(8,128)}, s32[]{:T(128)}) while((s32[]{:T(128)}, f32[32,16,512]{2,1,0:T(8,128)S(1)}, f32[4,32,16,512]{3,2,1,0:T(8,128)}, s32[]{:T(128)}) %tuple.163), condition=%wide.region_4.5_spmd, body=%wide.region_3.4_spmd.sunk | while | flops 8650754 | bytes 8388661 | solution.py:103
  201.7 3.9 collective-permute-start.8
  208.7 15.3 %collective-permute-done.8 = f32[8,16,512]{2,1,0:T(8,128)} collective-permute-done((f32[8,16,512]{2,1,0:T(8,128)S(1)}, f32[8,16,512]{2,1,0:T(8,128)}, u32[]{:S(2)}, u32[]{:S(2)}) %collective-permute-start.8) | collective-permute-done | bytes 262176 | tf_op jit(solution)/shard_map/ppermute | solution.py:18
  225.2 28.2 %while.37 = (s32[]{:T(128)}, f32[32,16,512]{2,1,0:T(8,128)S(1)}, f32[4,32,16,512]{3,2,1,0:T(8,128)}, s32[]{:T(128)}) while((s32[]{:T(128)}, f32[32,16,512]{2,1,0:T(8,128)S(1)}, f32[4,32,16,512]{3,2,1,0:T(8,128)}, s32[]{:T(128)}) %tuple.172), condition=%wide.region_6.7_spmd, body=%wide.region_5.6_spmd.sunk | while | flops 8650754 | bytes 8388661 | solution.py:103
  228.8 3.4 fusion.125
  232.3 3.4 fusion.125
  239.4 3.4 fusion.125
  242.9 3.4 fusion.125
  246.4 3.4 fusion.125
  254.4 19.2 %fusion.82 = f32[16,16,512]{2,1,0:T(8,128)S(1)} fusion(f32[18,18,514]{2,1,0:T(8,128)S(1)} %select_maximum_fusion.4, f32[1,16,512]{2,1,0:T(8,128)S(1)} %collective-permute-done.10, f32[16,16,512]{2,1,0:T(8,128)S(1)} %bitcast.237, f32[1,16,512]{2,1,0:T(8,128)S(1)} %collective-permute-done.9, f32[]{:T(128)} %bitcast.78, f32[]{:T(128)} %bitcast.77, ...), kind=kLoop, calls=%fused_computation.179 | loop fusion | flops 7340032 | bytes 14221420 | tf_op jit(solution)/shard_map/sub | solution.py:108
  273.7 769.2 %while.38 = (s32[]{:T(128)}, f32[16,16,512]{2,1,0:T(8,128)S(1)}, pred[]{:T(512)}, f32[3,3,3]{2,1,0:T(4,128)S(1)}, f32[16,16,512]{2,1,0:T(8,128)S(1)}, /*index=5*/f32[16,16,512]{2,1,0:T(8,128)S(1)}, s32[]{:T(128)}) while((s32[]{:T(128)}, f32[16,16,512]{2,1,0:T(8,128)S(1)}, pred[]{:T(512)}, f32[3,3,3]{2,1,0:T(4,128)S(1)}, ...), condition=%wide.region_8.9_spmd, body=%wide.region_7.8_spmd.sunk | while | flops 9969146 | bytes 18492456 | solution.py:116
  275.6 16.9 %collective-permute-start.1 = (f32[1,16,512]{2,1,0:T(8,128)S(1)}, f32[1,16,512]{2,1,0:T(8,128)S(1)}, u32[]{:S(2)}, u32[]{:S(2)}) collective-permute-start(f32[1,16,512]{2,1,0:T(8,128)S(1)} %get-tuple-element.401), channel_id=1, source_target_pairs={{0,1},{1,2},{2,3},{3,4},{4,5},{5,6},{6,7},{7,8},{8,9},{9,10},{10,1... | collective-permute-start | bytes 98312 | tf_op jit(solution)/shard_map/while/body/eval_jaxpr/ppermute | solution.py:17
  294.4 19.2 %fusion.129 = f32[16,16,512]{2,1,0:T(8,128)S(1)} fusion(f32[16,16,512]{2,1,0:T(8,128)S(1)} %get-tuple-element.472, f32[16,16,512]{2,1,0:T(8,128)S(1)} %get-tuple-element.471, f32[18,18,514]{2,1,0:T(8,128)S(1)} %select_maximum_fusion.7, f32[1,16,512]{2,1,0:T(8,128)S(1)} %collective-permute-done, f32[16,16,512]{2,1,0:T(8,128)S(1)} %get-tuple-element.461, ...), kind=kLoop, calls=%fused_computation.52.clone.1 | loop fusion | flops 7471104 | bytes 14745709 | tf_op jit(solution)/shard_map/while/body/eval_jaxpr/jit(_where)/select_n | solution.py:111
  315.6 8.6 collective-permute-done.2
  326.1 17.2 %collective-permute-start.1 = (f32[1,16,512]{2,1,0:T(8,128)S(1)}, f32[1,16,512]{2,1,0:T(8,128)S(1)}, u32[]{:S(2)}, u32[]{:S(2)}) collective-permute-start(f32[1,16,512]{2,1,0:T(8,128)S(1)} %get-tuple-element.401), channel_id=1, source_target_pairs={{0,1},{1,2},{2,3},{3,4},{4,5},{5,6},{6,7},{7,8},{8,9},{9,10},{10,1... | collective-permute-start | bytes 98312 | tf_op jit(solution)/shard_map/while/body/eval_jaxpr/ppermute | solution.py:17
  345.2 19.2 %fusion.129 = f32[16,16,512]{2,1,0:T(8,128)S(1)} fusion(f32[16,16,512]{2,1,0:T(8,128)S(1)} %get-tuple-element.472, f32[16,16,512]{2,1,0:T(8,128)S(1)} %get-tuple-element.471, f32[18,18,514]{2,1,0:T(8,128)S(1)} %select_maximum_fusion.7, f32[1,16,512]{2,1,0:T(8,128)S(1)} %collective-permute-done, f32[16,16,512]{2,1,0:T(8,128)S(1)} %get-tuple-element.461, ...), kind=kLoop, calls=%fused_computation.52.clone.1 | loop fusion | flops 7471104 | bytes 14745709 | tf_op jit(solution)/shard_map/while/body/eval_jaxpr/jit(_where)/select_n | solution.py:111
  366.3 8.6 collective-permute-done.2
  376.8 17.6 %collective-permute-start.1 = (f32[1,16,512]{2,1,0:T(8,128)S(1)}, f32[1,16,512]{2,1,0:T(8,128)S(1)}, u32[]{:S(2)}, u32[]{:S(2)}) collective-permute-start(f32[1,16,512]{2,1,0:T(8,128)S(1)} %get-tuple-element.401), channel_id=1, source_target_pairs={{0,1},{1,2},{2,3},{3,4},{4,5},{5,6},{6,7},{7,8},{8,9},{9,10},{10,1... | collective-permute-start | bytes 98312 | tf_op jit(solution)/shard_map/while/body/eval_jaxpr/ppermute | solution.py:17
  396.4 19.2 %fusion.129 = f32[16,16,512]{2,1,0:T(8,128)S(1)} fusion(f32[16,16,512]{2,1,0:T(8,128)S(1)} %get-tuple-element.472, f32[16,16,512]{2,1,0:T(8,128)S(1)} %get-tuple-element.471, f32[18,18,514]{2,1,0:T(8,128)S(1)} %select_maximum_fusion.7, f32[1,16,512]{2,1,0:T(8,128)S(1)} %collective-permute-done, f32[16,16,512]{2,1,0:T(8,128)S(1)} %get-tuple-element.461, ...), kind=kLoop, calls=%fused_computation.52.clone.1 | loop fusion | flops 7471104 | bytes 14745709 | tf_op jit(solution)/shard_map/while/body/eval_jaxpr/jit(_where)/select_n | solution.py:111
  417.6 8.6 collective-permute-done.2
  428.1 17.9 %collective-permute-start.1 = (f32[1,16,512]{2,1,0:T(8,128)S(1)}, f32[1,16,512]{2,1,0:T(8,128)S(1)}, u32[]{:S(2)}, u32[]{:S(2)}) collective-permute-start(f32[1,16,512]{2,1,0:T(8,128)S(1)} %get-tuple-element.401), channel_id=1, source_target_pairs={{0,1},{1,2},{2,3},{3,4},{4,5},{5,6},{6,7},{7,8},{8,9},{9,10},{10,1... | collective-permute-start | bytes 98312 | tf_op jit(solution)/shard_map/while/body/eval_jaxpr/ppermute | solution.py:17
  448.0 19.2 %fusion.129 = f32[16,16,512]{2,1,0:T(8,128)S(1)} fusion(f32[16,16,512]{2,1,0:T(8,128)S(1)} %get-tuple-element.472, f32[16,16,512]{2,1,0:T(8,128)S(1)} %get-tuple-element.471, f32[18,18,514]{2,1,0:T(8,128)S(1)} %select_maximum_fusion.7, f32[1,16,512]{2,1,0:T(8,128)S(1)} %collective-permute-done, f32[16,16,512]{2,1,0:T(8,128)S(1)} %get-tuple-element.461, ...), kind=kLoop, calls=%fused_computation.52.clone.1 | loop fusion | flops 7471104 | bytes 14745709 | tf_op jit(solution)/shard_map/while/body/eval_jaxpr/jit(_where)/select_n | solution.py:111
  469.1 8.6 collective-permute-done.2
  479.6 17.6 %collective-permute-start.1 = (f32[1,16,512]{2,1,0:T(8,128)S(1)}, f32[1,16,512]{2,1,0:T(8,128)S(1)}, u32[]{:S(2)}, u32[]{:S(2)}) collective-permute-start(f32[1,16,512]{2,1,0:T(8,128)S(1)} %get-tuple-element.401), channel_id=1, source_target_pairs={{0,1},{1,2},{2,3},{3,4},{4,5},{5,6},{6,7},{7,8},{8,9},{9,10},{10,1... | collective-permute-start | bytes 98312 | tf_op jit(solution)/shard_map/while/body/eval_jaxpr/ppermute | solution.py:17
  499.2 19.2 %fusion.129 = f32[16,16,512]{2,1,0:T(8,128)S(1)} fusion(f32[16,16,512]{2,1,0:T(8,128)S(1)} %get-tuple-element.472, f32[16,16,512]{2,1,0:T(8,128)S(1)} %get-tuple-element.471, f32[18,18,514]{2,1,0:T(8,128)S(1)} %select_maximum_fusion.7, f32[1,16,512]{2,1,0:T(8,128)S(1)} %collective-permute-done, f32[16,16,512]{2,1,0:T(8,128)S(1)} %get-tuple-element.461, ...), kind=kLoop, calls=%fused_computation.52.clone.1 | loop fusion | flops 7471104 | bytes 14745709 | tf_op jit(solution)/shard_map/while/body/eval_jaxpr/jit(_where)/select_n | solution.py:111
  520.4 8.6 collective-permute-done.2
  530.9 17.5 %collective-permute-start.1 = (f32[1,16,512]{2,1,0:T(8,128)S(1)}, f32[1,16,512]{2,1,0:T(8,128)S(1)}, u32[]{:S(2)}, u32[]{:S(2)}) collective-permute-start(f32[1,16,512]{2,1,0:T(8,128)S(1)} %get-tuple-element.401), channel_id=1, source_target_pairs={{0,1},{1,2},{2,3},{3,4},{4,5},{5,6},{6,7},{7,8},{8,9},{9,10},{10,1... | collective-permute-start | bytes 98312 | tf_op jit(solution)/shard_map/while/body/eval_jaxpr/ppermute | solution.py:17
  550.3 19.2 %fusion.129 = f32[16,16,512]{2,1,0:T(8,128)S(1)} fusion(f32[16,16,512]{2,1,0:T(8,128)S(1)} %get-tuple-element.472, f32[16,16,512]{2,1,0:T(8,128)S(1)} %get-tuple-element.471, f32[18,18,514]{2,1,0:T(8,128)S(1)} %select_maximum_fusion.7, f32[1,16,512]{2,1,0:T(8,128)S(1)} %collective-permute-done, f32[16,16,512]{2,1,0:T(8,128)S(1)} %get-tuple-element.461, ...), kind=kLoop, calls=%fused_computation.52.clone.1 | loop fusion | flops 7471104 | bytes 14745709 | tf_op jit(solution)/shard_map/while/body/eval_jaxpr/jit(_where)/select_n | solution.py:111
  571.5 8.6 collective-permute-done.2
  582.0 17.6 %collective-permute-start.1 = (f32[1,16,512]{2,1,0:T(8,128)S(1)}, f32[1,16,512]{2,1,0:T(8,128)S(1)}, u32[]{:S(2)}, u32[]{:S(2)}) collective-permute-start(f32[1,16,512]{2,1,0:T(8,128)S(1)} %get-tuple-element.401), channel_id=1, source_target_pairs={{0,1},{1,2},{2,3},{3,4},{4,5},{5,6},{6,7},{7,8},{8,9},{9,10},{10,1... | collective-permute-start | bytes 98312 | tf_op jit(solution)/shard_map/while/body/eval_jaxpr/ppermute | solution.py:17
  601.6 19.2 %fusion.129 = f32[16,16,512]{2,1,0:T(8,128)S(1)} fusion(f32[16,16,512]{2,1,0:T(8,128)S(1)} %get-tuple-element.472, f32[16,16,512]{2,1,0:T(8,128)S(1)} %get-tuple-element.471, f32[18,18,514]{2,1,0:T(8,128)S(1)} %select_maximum_fusion.7, f32[1,16,512]{2,1,0:T(8,128)S(1)} %collective-permute-done, f32[16,16,512]{2,1,0:T(8,128)S(1)} %get-tuple-element.461, ...), kind=kLoop, calls=%fused_computation.52.clone.1 | loop fusion | flops 7471104 | bytes 14745709 | tf_op jit(solution)/shard_map/while/body/eval_jaxpr/jit(_where)/select_n | solution.py:111
  622.7 8.6 collective-permute-done.2
  633.2 17.5 %collective-permute-start.1 = (f32[1,16,512]{2,1,0:T(8,128)S(1)}, f32[1,16,512]{2,1,0:T(8,128)S(1)}, u32[]{:S(2)}, u32[]{:S(2)}) collective-permute-start(f32[1,16,512]{2,1,0:T(8,128)S(1)} %get-tuple-element.401), channel_id=1, source_target_pairs={{0,1},{1,2},{2,3},{3,4},{4,5},{5,6},{6,7},{7,8},{8,9},{9,10},{10,1... | collective-permute-start | bytes 98312 | tf_op jit(solution)/shard_map/while/body/eval_jaxpr/ppermute | solution.py:17
  652.9 19.2 %fusion.129 = f32[16,16,512]{2,1,0:T(8,128)S(1)} fusion(f32[16,16,512]{2,1,0:T(8,128)S(1)} %get-tuple-element.472, f32[16,16,512]{2,1,0:T(8,128)S(1)} %get-tuple-element.471, f32[18,18,514]{2,1,0:T(8,128)S(1)} %select_maximum_fusion.7, f32[1,16,512]{2,1,0:T(8,128)S(1)} %collective-permute-done, f32[16,16,512]{2,1,0:T(8,128)S(1)} %get-tuple-element.461, ...), kind=kLoop, calls=%fused_computation.52.clone.1 | loop fusion | flops 7471104 | bytes 14745709 | tf_op jit(solution)/shard_map/while/body/eval_jaxpr/jit(_where)/select_n | solution.py:111
  674.1 8.6 collective-permute-done.2
  684.5 17.6 %collective-permute-start.1 = (f32[1,16,512]{2,1,0:T(8,128)S(1)}, f32[1,16,512]{2,1,0:T(8,128)S(1)}, u32[]{:S(2)}, u32[]{:S(2)}) collective-permute-start(f32[1,16,512]{2,1,0:T(8,128)S(1)} %get-tuple-element.401), channel_id=1, source_target_pairs={{0,1},{1,2},{2,3},{3,4},{4,5},{5,6},{6,7},{7,8},{8,9},{9,10},{10,1... | collective-permute-start | bytes 98312 | tf_op jit(solution)/shard_map/while/body/eval_jaxpr/ppermute | solution.py:17
  704.4 19.2 %fusion.129 = f32[16,16,512]{2,1,0:T(8,128)S(1)} fusion(f32[16,16,512]{2,1,0:T(8,128)S(1)} %get-tuple-element.472, f32[16,16,512]{2,1,0:T(8,128)S(1)} %get-tuple-element.471, f32[18,18,514]{2,1,0:T(8,128)S(1)} %select_maximum_fusion.7, f32[1,16,512]{2,1,0:T(8,128)S(1)} %collective-permute-done, f32[16,16,512]{2,1,0:T(8,128)S(1)} %get-tuple-element.461, ...), kind=kLoop, calls=%fused_computation.52.clone.1 | loop fusion | flops 7471104 | bytes 14745709 | tf_op jit(solution)/shard_map/while/body/eval_jaxpr/jit(_where)/select_n | solution.py:111
  725.5 8.6 collective-permute-done.2
  736.0 17.6 %collective-permute-start.1 = (f32[1,16,512]{2,1,0:T(8,128)S(1)}, f32[1,16,512]{2,1,0:T(8,128)S(1)}, u32[]{:S(2)}, u32[]{:S(2)}) collective-permute-start(f32[1,16,512]{2,1,0:T(8,128)S(1)} %get-tuple-element.401), channel_id=1, source_target_pairs={{0,1},{1,2},{2,3},{3,4},{4,5},{5,6},{6,7},{7,8},{8,9},{9,10},{10,1... | collective-permute-start | bytes 98312 | tf_op jit(solution)/shard_map/while/body/eval_jaxpr/ppermute | solution.py:17
  755.8 19.2 %fusion.129 = f32[16,16,512]{2,1,0:T(8,128)S(1)} fusion(f32[16,16,512]{2,1,0:T(8,128)S(1)} %get-tuple-element.472, f32[16,16,512]{2,1,0:T(8,128)S(1)} %get-tuple-element.471, f32[18,18,514]{2,1,0:T(8,128)S(1)} %select_maximum_fusion.7, f32[1,16,512]{2,1,0:T(8,128)S(1)} %collective-permute-done, f32[16,16,512]{2,1,0:T(8,128)S(1)} %get-tuple-element.461, ...), kind=kLoop, calls=%fused_computation.52.clone.1 | loop fusion | flops 7471104 | bytes 14745709 | tf_op jit(solution)/shard_map/while/body/eval_jaxpr/jit(_where)/select_n | solution.py:111
  777.0 8.6 collective-permute-done.2
  787.5 17.6 %collective-permute-start.1 = (f32[1,16,512]{2,1,0:T(8,128)S(1)}, f32[1,16,512]{2,1,0:T(8,128)S(1)}, u32[]{:S(2)}, u32[]{:S(2)}) collective-permute-start(f32[1,16,512]{2,1,0:T(8,128)S(1)} %get-tuple-element.401), channel_id=1, source_target_pairs={{0,1},{1,2},{2,3},{3,4},{4,5},{5,6},{6,7},{7,8},{8,9},{9,10},{10,1... | collective-permute-start | bytes 98312 | tf_op jit(solution)/shard_map/while/body/eval_jaxpr/ppermute | solution.py:17
  807.3 19.2 %fusion.129 = f32[16,16,512]{2,1,0:T(8,128)S(1)} fusion(f32[16,16,512]{2,1,0:T(8,128)S(1)} %get-tuple-element.472, f32[16,16,512]{2,1,0:T(8,128)S(1)} %get-tuple-element.471, f32[18,18,514]{2,1,0:T(8,128)S(1)} %select_maximum_fusion.7, f32[1,16,512]{2,1,0:T(8,128)S(1)} %collective-permute-done, f32[16,16,512]{2,1,0:T(8,128)S(1)} %get-tuple-element.461, ...), kind=kLoop, calls=%fused_computation.52.clone.1 | loop fusion | flops 7471104 | bytes 14745709 | tf_op jit(solution)/shard_map/while/body/eval_jaxpr/jit(_where)/select_n | solution.py:111
  828.4 8.6 collective-permute-done.2
  838.9 17.6 %collective-permute-start.1 = (f32[1,16,512]{2,1,0:T(8,128)S(1)}, f32[1,16,512]{2,1,0:T(8,128)S(1)}, u32[]{:S(2)}, u32[]{:S(2)}) collective-permute-start(f32[1,16,512]{2,1,0:T(8,128)S(1)} %get-tuple-element.401), channel_id=1, source_target_pairs={{0,1},{1,2},{2,3},{3,4},{4,5},{5,6},{6,7},{7,8},{8,9},{9,10},{10,1... | collective-permute-start | bytes 98312 | tf_op jit(solution)/shard_map/while/body/eval_jaxpr/ppermute | solution.py:17
  858.7 19.2 %fusion.129 = f32[16,16,512]{2,1,0:T(8,128)S(1)} fusion(f32[16,16,512]{2,1,0:T(8,128)S(1)} %get-tuple-element.472, f32[16,16,512]{2,1,0:T(8,128)S(1)} %get-tuple-element.471, f32[18,18,514]{2,1,0:T(8,128)S(1)} %select_maximum_fusion.7, f32[1,16,512]{2,1,0:T(8,128)S(1)} %collective-permute-done, f32[16,16,512]{2,1,0:T(8,128)S(1)} %get-tuple-element.461, ...), kind=kLoop, calls=%fused_computation.52.clone.1 | loop fusion | flops 7471104 | bytes 14745709 | tf_op jit(solution)/shard_map/while/body/eval_jaxpr/jit(_where)/select_n | solution.py:111
  879.9 8.6 collective-permute-done.2
  890.4 17.6 %collective-permute-start.1 = (f32[1,16,512]{2,1,0:T(8,128)S(1)}, f32[1,16,512]{2,1,0:T(8,128)S(1)}, u32[]{:S(2)}, u32[]{:S(2)}) collective-permute-start(f32[1,16,512]{2,1,0:T(8,128)S(1)} %get-tuple-element.401), channel_id=1, source_target_pairs={{0,1},{1,2},{2,3},{3,4},{4,5},{5,6},{6,7},{7,8},{8,9},{9,10},{10,1... | collective-permute-start | bytes 98312 | tf_op jit(solution)/shard_map/while/body/eval_jaxpr/ppermute | solution.py:17
  910.2 19.2 %fusion.129 = f32[16,16,512]{2,1,0:T(8,128)S(1)} fusion(f32[16,16,512]{2,1,0:T(8,128)S(1)} %get-tuple-element.472, f32[16,16,512]{2,1,0:T(8,128)S(1)} %get-tuple-element.471, f32[18,18,514]{2,1,0:T(8,128)S(1)} %select_maximum_fusion.7, f32[1,16,512]{2,1,0:T(8,128)S(1)} %collective-permute-done, f32[16,16,512]{2,1,0:T(8,128)S(1)} %get-tuple-element.461, ...), kind=kLoop, calls=%fused_computation.52.clone.1 | loop fusion | flops 7471104 | bytes 14745709 | tf_op jit(solution)/shard_map/while/body/eval_jaxpr/jit(_where)/select_n | solution.py:111
  931.3 8.6 collective-permute-done.2
  941.8 17.6 %collective-permute-start.1 = (f32[1,16,512]{2,1,0:T(8,128)S(1)}, f32[1,16,512]{2,1,0:T(8,128)S(1)}, u32[]{:S(2)}, u32[]{:S(2)}) collective-permute-start(f32[1,16,512]{2,1,0:T(8,128)S(1)} %get-tuple-element.401), channel_id=1, source_target_pairs={{0,1},{1,2},{2,3},{3,4},{4,5},{5,6},{6,7},{7,8},{8,9},{9,10},{10,1... | collective-permute-start | bytes 98312 | tf_op jit(solution)/shard_map/while/body/eval_jaxpr/ppermute | solution.py:17
  961.7 19.2 %fusion.129 = f32[16,16,512]{2,1,0:T(8,128)S(1)} fusion(f32[16,16,512]{2,1,0:T(8,128)S(1)} %get-tuple-element.472, f32[16,16,512]{2,1,0:T(8,128)S(1)} %get-tuple-element.471, f32[18,18,514]{2,1,0:T(8,128)S(1)} %select_maximum_fusion.7, f32[1,16,512]{2,1,0:T(8,128)S(1)} %collective-permute-done, f32[16,16,512]{2,1,0:T(8,128)S(1)} %get-tuple-element.461, ...), kind=kLoop, calls=%fused_computation.52.clone.1 | loop fusion | flops 7471104 | bytes 14745709 | tf_op jit(solution)/shard_map/while/body/eval_jaxpr/jit(_where)/select_n | solution.py:111
  982.8 8.6 collective-permute-done.2
  993.3 17.6 %collective-permute-start.1 = (f32[1,16,512]{2,1,0:T(8,128)S(1)}, f32[1,16,512]{2,1,0:T(8,128)S(1)}, u32[]{:S(2)}, u32[]{:S(2)}) collective-permute-start(f32[1,16,512]{2,1,0:T(8,128)S(1)} %get-tuple-element.401), channel_id=1, source_target_pairs={{0,1},{1,2},{2,3},{3,4},{4,5},{5,6},{6,7},{7,8},{8,9},{9,10},{10,1... | collective-permute-start | bytes 98312 | tf_op jit(solution)/shard_map/while/body/eval_jaxpr/ppermute | solution.py:17
  1013.1 19.2 %fusion.129 = f32[16,16,512]{2,1,0:T(8,128)S(1)} fusion(f32[16,16,512]{2,1,0:T(8,128)S(1)} %get-tuple-element.472, f32[16,16,512]{2,1,0:T(8,128)S(1)} %get-tuple-element.471, f32[18,18,514]{2,1,0:T(8,128)S(1)} %select_maximum_fusion.7, f32[1,16,512]{2,1,0:T(8,128)S(1)} %collective-permute-done, f32[16,16,512]{2,1,0:T(8,128)S(1)} %get-tuple-element.461, ...), kind=kLoop, calls=%fused_computation.52.clone.1 | loop fusion | flops 7471104 | bytes 14745709 | tf_op jit(solution)/shard_map/while/body/eval_jaxpr/jit(_where)/select_n | solution.py:111
  1034.3 8.6 collective-permute-done.2
  1042.8 17.3 %collective-permute-start.11 = (f32[1,16,512]{2,1,0:T(8,128)S(1)}, f32[1,16,512]{2,1,0:T(8,128)S(1)}, u32[]{:S(2)}, u32[]{:S(2)}) collective-permute-start(f32[1,16,512]{2,1,0:T(8,128)S(1)} %get-tuple-element.245), channel_id=1, source_target_pairs={{0,1},{1,2},{2,3},{3,4},{4,5},{5,6},{6,7},{7,8},{8,9},{9,10},{10,1... | collective-permute-start | bytes 98312 | tf_op jit(solution)/shard_map/ppermute | solution.py:17
  1062.1 16.8 %collective-permute-done.12 = f32[1,16,512]{2,1,0:T(8,128)S(1)} collective-permute-done((f32[1,16,512]{2,1,0:T(8,128)S(1)}, f32[1,16,512]{2,1,0:T(8,128)S(1)}, u32[]{:S(2)}, u32[]{:S(2)}) %collective-permute-start.12) | collective-permute-done | bytes 32800 | tf_op jit(solution)/shard_map/ppermute | solution.py:18
  1079.2 19.9 %fusion.53 = f32[1,16,16,512]{3,2,1,0:T(8,128)} fusion(f32[16,16,512]{2,1,0:T(8,128)S(1)} %get-tuple-element.476, f32[18,18,514]{2,1,0:T(8,128)S(1)} %select_maximum_fusion.2, f32[1,16,512]{2,1,0:T(8,128)S(1)} %collective-permute-done.12, f32[16,16,512]{2,1,0:T(8,128)S(1)} %get-tuple-element.168, f32[1,16,512]{2,1,0:T(8,128)S(1)} %collective-permute-done.11, ...), kind=kLoop, calls=%fused_computation.124 | loop fusion | flops 7471104 | bytes 14745709 | tf_op jit(solution)/shard_map/broadcast_in_dim | solution.py:118
  (189 shorter events, 153.8 us)
Async XLA Ops:
  8.2 1.7 copy-start
  8.2 18.0 %copy-start.2 = (f32[1,16,16,512]{3,2,1,0:T(8,128)S(1)}, f32[1,16,16,512]{3,2,1,0:T(8,128)}, u32[]{:S(2)}) copy-start(f32[1,16,16,512]{3,2,1,0:T(8,128)} %param.13) | copy-start | bytes 1572868
  8.2 36.9 %copy-start.4 = (f32[3,3,3]{2,1,0:T(4,128)S(1)}, f32[3,3,3]{2,1,0:T(4,128)}, u32[]{:S(2)}) copy-start(f32[3,3,3]{2,1,0:T(4,128)} %param.19) | copy-start | bytes 328
  9.9 157.7 %collective-permute-start.5 = (f32[4,8,16,512]{3,2,1,0:T(8,128)}, f32[4,8,16,512]{3,2,1,0:T(8,128)}, u32[]{:S(2)}, u32[]{:S(2)}) collective-permute-start(f32[4,8,16,512]{3,2,1,0:T(8,128)} %get-tuple-element.241), channel_id=1, source_target_pairs={{0,1},{1,2},{2,3},{3,4},{4,5},{5,6},{6,7},{7,8},{8,9},{9,10},{10,1... | collective-permute-start | bytes 3145736 | tf_op jit(solution)/shard_map/ppermute | solution.py:17
  24.3 143.3 %collective-permute-start.6 = (f32[4,8,16,512]{3,2,1,0:T(8,128)S(1)}, f32[4,8,16,512]{3,2,1,0:T(8,128)}, u32[]{:S(2)}, u32[]{:S(2)}) collective-permute-start(f32[4,8,16,512]{3,2,1,0:T(8,128)S(1)} %get-tuple-element.242), channel_id=1, source_target_pairs={{1,0},{2,1},{3,2},{4,3},{5,4},{6,5},{7,6},{8,7},{9,8},{10,9},{11,1... | collective-permute-start | bytes 3145736 | tf_op jit(solution)/shard_map/ppermute | solution.py:18
  26.3 123.8 %collective-permute-start.3 = (f32[8,16,512]{2,1,0:T(8,128)S(1)}, f32[8,16,512]{2,1,0:T(8,128)S(1)}, u32[]{:S(2)}, u32[]{:S(2)}) collective-permute-start(f32[8,16,512]{2,1,0:T(8,128)S(1)} %get-tuple-element.263), channel_id=1, source_target_pairs={{0,1},{1,2},{2,3},{3,4},{4,5},{5,6},{6,7},{7,8},{8,9},{9,10},{10,1... | collective-permute-start | bytes 786440 | tf_op jit(solution)/shard_map/ppermute | solution.py:17
  43.1 124.3 %collective-permute-start.4 = (f32[8,16,512]{2,1,0:T(8,128)S(1)}, f32[8,16,512]{2,1,0:T(8,128)S(1)}, u32[]{:S(2)}, u32[]{:S(2)}) collective-permute-start(f32[8,16,512]{2,1,0:T(8,128)S(1)} %get-tuple-element.264), channel_id=1, source_target_pairs={{1,0},{2,1},{3,2},{4,3},{5,4},{6,5},{7,6},{8,7},{9,8},{10,9},{11,1... | collective-permute-start | bytes 786440 | tf_op jit(solution)/shard_map/ppermute | solution.py:18
  45.8 121.8 %copy-start.1 = (f32[4,16,16,512]{3,2,1,0:T(8,128)S(1)}, f32[4,16,16,512]{3,2,1,0:T(8,128)}, u32[]{:S(2)}) copy-start(f32[4,16,16,512]{3,2,1,0:T(8,128)} %copy-done) | copy-start | bytes 6291460
  46.4 160.0 %collective-permute-start.10 = (f32[1,16,512]{2,1,0:T(8,128)}, f32[1,16,512]{2,1,0:T(8,128)S(1)}, u32[]{:S(2)}, u32[]{:S(2)}) collective-permute-start(f32[1,16,512]{2,1,0:T(8,128)} %get-tuple-element.266), channel_id=1, source_target_pairs={{1,0},{2,1},{3,2},{4,3},{5,4},{6,5},{7,6},{8,7},{9,8},{10,9},{11,1... | collective-permute-start | bytes 98312 | tf_op jit(solution)/shard_map/ppermute | solution.py:18
  150.1 56.3 %collective-permute-start.9 = (f32[1,16,512]{2,1,0:T(8,128)S(1)}, f32[1,16,512]{2,1,0:T(8,128)S(1)}, u32[]{:S(2)}, u32[]{:S(2)}) collective-permute-start(f32[1,16,512]{2,1,0:T(8,128)S(1)} %get-tuple-element.265), channel_id=1, source_target_pairs={{0,1},{1,2},{2,3},{3,4},{4,5},{5,6},{6,7},{7,8},{8,9},{9,10},{10,1... | collective-permute-start | bytes 98312 | tf_op jit(solution)/shard_map/ppermute | solution.py:17
  199.8 8.9 collective-permute-start.7
  201.7 22.3 %collective-permute-start.8 = (f32[8,16,512]{2,1,0:T(8,128)S(1)}, f32[8,16,512]{2,1,0:T(8,128)}, u32[]{:S(2)}, u32[]{:S(2)}) collective-permute-start(f32[8,16,512]{2,1,0:T(8,128)S(1)} %get-tuple-element.244), channel_id=1, source_target_pairs={{1,0},{2,1},{3,2},{4,3},{5,4},{6,5},{7,6},{8,7},{9,8},{10,9},{11,1... | collective-permute-start | bytes 786440 | tf_op jit(solution)/shard_map/ppermute | solution.py:18
  253.3 1.0 copy-start.3
  273.7 20.2 %collective-permute-start = (f32[1,16,512]{2,1,0:T(8,128)S(1)}, f32[1,16,512]{2,1,0:T(8,128)S(1)}, u32[]{:S(2)}, u32[]{:S(2)}) collective-permute-start(f32[1,16,512]{2,1,0:T(8,128)S(1)} %get-tuple-element.400), channel_id=1, source_target_pairs={{1,0},{2,1},{3,2},{4,3},{5,4},{6,5},{7,6},{8,7},{9,8},{10,9},{11,1... | collective-permute-start | bytes 98312 | tf_op jit(solution)/shard_map/while/body/eval_jaxpr/ppermute | solution.py:18
  275.6 18.4 %collective-permute-start.1 = (f32[1,16,512]{2,1,0:T(8,128)S(1)}, f32[1,16,512]{2,1,0:T(8,128)S(1)}, u32[]{:S(2)}, u32[]{:S(2)}) collective-permute-start(f32[1,16,512]{2,1,0:T(8,128)S(1)} %get-tuple-element.401), channel_id=1, source_target_pairs={{0,1},{1,2},{2,3},{3,4},{4,5},{5,6},{6,7},{7,8},{8,9},{9,10},{10,1... | collective-permute-start | bytes 98312 | tf_op jit(solution)/shard_map/while/body/eval_jaxpr/ppermute | solution.py:17
  313.6 10.5 collective-permute-start.2
  324.2 20.5 %collective-permute-start = (f32[1,16,512]{2,1,0:T(8,128)S(1)}, f32[1,16,512]{2,1,0:T(8,128)S(1)}, u32[]{:S(2)}, u32[]{:S(2)}) collective-permute-start(f32[1,16,512]{2,1,0:T(8,128)S(1)} %get-tuple-element.400), channel_id=1, source_target_pairs={{1,0},{2,1},{3,2},{4,3},{5,4},{6,5},{7,6},{8,7},{9,8},{10,9},{11,1... | collective-permute-start | bytes 98312 | tf_op jit(solution)/shard_map/while/body/eval_jaxpr/ppermute | solution.py:18
  326.1 18.7 %collective-permute-start.1 = (f32[1,16,512]{2,1,0:T(8,128)S(1)}, f32[1,16,512]{2,1,0:T(8,128)S(1)}, u32[]{:S(2)}, u32[]{:S(2)}) collective-permute-start(f32[1,16,512]{2,1,0:T(8,128)S(1)} %get-tuple-element.401), channel_id=1, source_target_pairs={{0,1},{1,2},{2,3},{3,4},{4,5},{5,6},{6,7},{7,8},{8,9},{9,10},{10,1... | collective-permute-start | bytes 98312 | tf_op jit(solution)/shard_map/while/body/eval_jaxpr/ppermute | solution.py:17
  364.4 10.5 collective-permute-start.2
  374.9 21.0 %collective-permute-start = (f32[1,16,512]{2,1,0:T(8,128)S(1)}, f32[1,16,512]{2,1,0:T(8,128)S(1)}, u32[]{:S(2)}, u32[]{:S(2)}) collective-permute-start(f32[1,16,512]{2,1,0:T(8,128)S(1)} %get-tuple-element.400), channel_id=1, source_target_pairs={{1,0},{2,1},{3,2},{4,3},{5,4},{6,5},{7,6},{8,7},{9,8},{10,9},{11,1... | collective-permute-start | bytes 98312 | tf_op jit(solution)/shard_map/while/body/eval_jaxpr/ppermute | solution.py:18
  376.8 19.2 %collective-permute-start.1 = (f32[1,16,512]{2,1,0:T(8,128)S(1)}, f32[1,16,512]{2,1,0:T(8,128)S(1)}, u32[]{:S(2)}, u32[]{:S(2)}) collective-permute-start(f32[1,16,512]{2,1,0:T(8,128)S(1)} %get-tuple-element.401), channel_id=1, source_target_pairs={{0,1},{1,2},{2,3},{3,4},{4,5},{5,6},{6,7},{7,8},{8,9},{9,10},{10,1... | collective-permute-start | bytes 98312 | tf_op jit(solution)/shard_map/while/body/eval_jaxpr/ppermute | solution.py:17
  415.6 10.5 collective-permute-start.2
  426.2 21.2 %collective-permute-start = (f32[1,16,512]{2,1,0:T(8,128)S(1)}, f32[1,16,512]{2,1,0:T(8,128)S(1)}, u32[]{:S(2)}, u32[]{:S(2)}) collective-permute-start(f32[1,16,512]{2,1,0:T(8,128)S(1)} %get-tuple-element.400), channel_id=1, source_target_pairs={{1,0},{2,1},{3,2},{4,3},{5,4},{6,5},{7,6},{8,7},{9,8},{10,9},{11,1... | collective-permute-start | bytes 98312 | tf_op jit(solution)/shard_map/while/body/eval_jaxpr/ppermute | solution.py:18
  428.1 19.5 %collective-permute-start.1 = (f32[1,16,512]{2,1,0:T(8,128)S(1)}, f32[1,16,512]{2,1,0:T(8,128)S(1)}, u32[]{:S(2)}, u32[]{:S(2)}) collective-permute-start(f32[1,16,512]{2,1,0:T(8,128)S(1)} %get-tuple-element.401), channel_id=1, source_target_pairs={{0,1},{1,2},{2,3},{3,4},{4,5},{5,6},{6,7},{7,8},{8,9},{9,10},{10,1... | collective-permute-start | bytes 98312 | tf_op jit(solution)/shard_map/while/body/eval_jaxpr/ppermute | solution.py:17
  467.2 10.5 collective-permute-start.2
  477.7 21.0 %collective-permute-start = (f32[1,16,512]{2,1,0:T(8,128)S(1)}, f32[1,16,512]{2,1,0:T(8,128)S(1)}, u32[]{:S(2)}, u32[]{:S(2)}) collective-permute-start(f32[1,16,512]{2,1,0:T(8,128)S(1)} %get-tuple-element.400), channel_id=1, source_target_pairs={{1,0},{2,1},{3,2},{4,3},{5,4},{6,5},{7,6},{8,7},{9,8},{10,9},{11,1... | collective-permute-start | bytes 98312 | tf_op jit(solution)/shard_map/while/body/eval_jaxpr/ppermute | solution.py:18
  479.6 19.2 %collective-permute-start.1 = (f32[1,16,512]{2,1,0:T(8,128)S(1)}, f32[1,16,512]{2,1,0:T(8,128)S(1)}, u32[]{:S(2)}, u32[]{:S(2)}) collective-permute-start(f32[1,16,512]{2,1,0:T(8,128)S(1)} %get-tuple-element.401), channel_id=1, source_target_pairs={{0,1},{1,2},{2,3},{3,4},{4,5},{5,6},{6,7},{7,8},{8,9},{9,10},{10,1... | collective-permute-start | bytes 98312 | tf_op jit(solution)/shard_map/while/body/eval_jaxpr/ppermute | solution.py:17
  518.4 10.5 collective-permute-start.2
  529.0 20.8 %collective-permute-start = (f32[1,16,512]{2,1,0:T(8,128)S(1)}, f32[1,16,512]{2,1,0:T(8,128)S(1)}, u32[]{:S(2)}, u32[]{:S(2)}) collective-permute-start(f32[1,16,512]{2,1,0:T(8,128)S(1)} %get-tuple-element.400), channel_id=1, source_target_pairs={{1,0},{2,1},{3,2},{4,3},{5,4},{6,5},{7,6},{8,7},{9,8},{10,9},{11,1... | collective-permute-start | bytes 98312 | tf_op jit(solution)/shard_map/while/body/eval_jaxpr/ppermute | solution.py:18
  530.9 19.1 %collective-permute-start.1 = (f32[1,16,512]{2,1,0:T(8,128)S(1)}, f32[1,16,512]{2,1,0:T(8,128)S(1)}, u32[]{:S(2)}, u32[]{:S(2)}) collective-permute-start(f32[1,16,512]{2,1,0:T(8,128)S(1)} %get-tuple-element.401), channel_id=1, source_target_pairs={{0,1},{1,2},{2,3},{3,4},{4,5},{5,6},{6,7},{7,8},{8,9},{9,10},{10,1... | collective-permute-start | bytes 98312 | tf_op jit(solution)/shard_map/while/body/eval_jaxpr/ppermute | solution.py:17
  569.6 10.5 collective-permute-start.2
  580.1 21.0 %collective-permute-start = (f32[1,16,512]{2,1,0:T(8,128)S(1)}, f32[1,16,512]{2,1,0:T(8,128)S(1)}, u32[]{:S(2)}, u32[]{:S(2)}) collective-permute-start(f32[1,16,512]{2,1,0:T(8,128)S(1)} %get-tuple-element.400), channel_id=1, source_target_pairs={{1,0},{2,1},{3,2},{4,3},{5,4},{6,5},{7,6},{8,7},{9,8},{10,9},{11,1... | collective-permute-start | bytes 98312 | tf_op jit(solution)/shard_map/while/body/eval_jaxpr/ppermute | solution.py:18
  582.0 19.2 %collective-permute-start.1 = (f32[1,16,512]{2,1,0:T(8,128)S(1)}, f32[1,16,512]{2,1,0:T(8,128)S(1)}, u32[]{:S(2)}, u32[]{:S(2)}) collective-permute-start(f32[1,16,512]{2,1,0:T(8,128)S(1)} %get-tuple-element.401), channel_id=1, source_target_pairs={{0,1},{1,2},{2,3},{3,4},{4,5},{5,6},{6,7},{7,8},{8,9},{9,10},{10,1... | collective-permute-start | bytes 98312 | tf_op jit(solution)/shard_map/while/body/eval_jaxpr/ppermute | solution.py:17
  620.8 10.5 collective-permute-start.2
  631.3 20.8 %collective-permute-start = (f32[1,16,512]{2,1,0:T(8,128)S(1)}, f32[1,16,512]{2,1,0:T(8,128)S(1)}, u32[]{:S(2)}, u32[]{:S(2)}) collective-permute-start(f32[1,16,512]{2,1,0:T(8,128)S(1)} %get-tuple-element.400), channel_id=1, source_target_pairs={{1,0},{2,1},{3,2},{4,3},{5,4},{6,5},{7,6},{8,7},{9,8},{10,9},{11,1... | collective-permute-start | bytes 98312 | tf_op jit(solution)/shard_map/while/body/eval_jaxpr/ppermute | solution.py:18
  633.2 19.3 %collective-permute-start.1 = (f32[1,16,512]{2,1,0:T(8,128)S(1)}, f32[1,16,512]{2,1,0:T(8,128)S(1)}, u32[]{:S(2)}, u32[]{:S(2)}) collective-permute-start(f32[1,16,512]{2,1,0:T(8,128)S(1)} %get-tuple-element.401), channel_id=1, source_target_pairs={{0,1},{1,2},{2,3},{3,4},{4,5},{5,6},{6,7},{7,8},{8,9},{9,10},{10,1... | collective-permute-start | bytes 98312 | tf_op jit(solution)/shard_map/while/body/eval_jaxpr/ppermute | solution.py:17
  672.1 10.5 collective-permute-start.2
  682.6 21.0 %collective-permute-start = (f32[1,16,512]{2,1,0:T(8,128)S(1)}, f32[1,16,512]{2,1,0:T(8,128)S(1)}, u32[]{:S(2)}, u32[]{:S(2)}) collective-permute-start(f32[1,16,512]{2,1,0:T(8,128)S(1)} %get-tuple-element.400), channel_id=1, source_target_pairs={{1,0},{2,1},{3,2},{4,3},{5,4},{6,5},{7,6},{8,7},{9,8},{10,9},{11,1... | collective-permute-start | bytes 98312 | tf_op jit(solution)/shard_map/while/body/eval_jaxpr/ppermute | solution.py:18
  684.5 19.4 %collective-permute-start.1 = (f32[1,16,512]{2,1,0:T(8,128)S(1)}, f32[1,16,512]{2,1,0:T(8,128)S(1)}, u32[]{:S(2)}, u32[]{:S(2)}) collective-permute-start(f32[1,16,512]{2,1,0:T(8,128)S(1)} %get-tuple-element.401), channel_id=1, source_target_pairs={{0,1},{1,2},{2,3},{3,4},{4,5},{5,6},{6,7},{7,8},{8,9},{9,10},{10,1... | collective-permute-start | bytes 98312 | tf_op jit(solution)/shard_map/while/body/eval_jaxpr/ppermute | solution.py:17
  723.6 10.5 collective-permute-start.2
  734.1 21.0 %collective-permute-start = (f32[1,16,512]{2,1,0:T(8,128)S(1)}, f32[1,16,512]{2,1,0:T(8,128)S(1)}, u32[]{:S(2)}, u32[]{:S(2)}) collective-permute-start(f32[1,16,512]{2,1,0:T(8,128)S(1)} %get-tuple-element.400), channel_id=1, source_target_pairs={{1,0},{2,1},{3,2},{4,3},{5,4},{6,5},{7,6},{8,7},{9,8},{10,9},{11,1... | collective-permute-start | bytes 98312 | tf_op jit(solution)/shard_map/while/body/eval_jaxpr/ppermute | solution.py:18
  736.0 19.4 %collective-permute-start.1 = (f32[1,16,512]{2,1,0:T(8,128)S(1)}, f32[1,16,512]{2,1,0:T(8,128)S(1)}, u32[]{:S(2)}, u32[]{:S(2)}) collective-permute-start(f32[1,16,512]{2,1,0:T(8,128)S(1)} %get-tuple-element.401), channel_id=1, source_target_pairs={{0,1},{1,2},{2,3},{3,4},{4,5},{5,6},{6,7},{7,8},{8,9},{9,10},{10,1... | collective-permute-start | bytes 98312 | tf_op jit(solution)/shard_map/while/body/eval_jaxpr/ppermute | solution.py:17
  775.0 10.5 collective-permute-start.2
  785.5 21.0 %collective-permute-start = (f32[1,16,512]{2,1,0:T(8,128)S(1)}, f32[1,16,512]{2,1,0:T(8,128)S(1)}, u32[]{:S(2)}, u32[]{:S(2)}) collective-permute-start(f32[1,16,512]{2,1,0:T(8,128)S(1)} %get-tuple-element.400), channel_id=1, source_target_pairs={{1,0},{2,1},{3,2},{4,3},{5,4},{6,5},{7,6},{8,7},{9,8},{10,9},{11,1... | collective-permute-start | bytes 98312 | tf_op jit(solution)/shard_map/while/body/eval_jaxpr/ppermute | solution.py:18
  787.5 19.4 %collective-permute-start.1 = (f32[1,16,512]{2,1,0:T(8,128)S(1)}, f32[1,16,512]{2,1,0:T(8,128)S(1)}, u32[]{:S(2)}, u32[]{:S(2)}) collective-permute-start(f32[1,16,512]{2,1,0:T(8,128)S(1)} %get-tuple-element.401), channel_id=1, source_target_pairs={{0,1},{1,2},{2,3},{3,4},{4,5},{5,6},{6,7},{7,8},{8,9},{9,10},{10,1... | collective-permute-start | bytes 98312 | tf_op jit(solution)/shard_map/while/body/eval_jaxpr/ppermute | solution.py:17
  826.5 10.5 collective-permute-start.2
  837.0 21.0 %collective-permute-start = (f32[1,16,512]{2,1,0:T(8,128)S(1)}, f32[1,16,512]{2,1,0:T(8,128)S(1)}, u32[]{:S(2)}, u32[]{:S(2)}) collective-permute-start(f32[1,16,512]{2,1,0:T(8,128)S(1)} %get-tuple-element.400), channel_id=1, source_target_pairs={{1,0},{2,1},{3,2},{4,3},{5,4},{6,5},{7,6},{8,7},{9,8},{10,9},{11,1... | collective-permute-start | bytes 98312 | tf_op jit(solution)/shard_map/while/body/eval_jaxpr/ppermute | solution.py:18
  838.9 19.4 %collective-permute-start.1 = (f32[1,16,512]{2,1,0:T(8,128)S(1)}, f32[1,16,512]{2,1,0:T(8,128)S(1)}, u32[]{:S(2)}, u32[]{:S(2)}) collective-permute-start(f32[1,16,512]{2,1,0:T(8,128)S(1)} %get-tuple-element.401), channel_id=1, source_target_pairs={{0,1},{1,2},{2,3},{3,4},{4,5},{5,6},{6,7},{7,8},{8,9},{9,10},{10,1... | collective-permute-start | bytes 98312 | tf_op jit(solution)/shard_map/while/body/eval_jaxpr/ppermute | solution.py:17
  878.0 10.5 collective-permute-start.2
  888.5 21.0 %collective-permute-start = (f32[1,16,512]{2,1,0:T(8,128)S(1)}, f32[1,16,512]{2,1,0:T(8,128)S(1)}, u32[]{:S(2)}, u32[]{:S(2)}) collective-permute-start(f32[1,16,512]{2,1,0:T(8,128)S(1)} %get-tuple-element.400), channel_id=1, source_target_pairs={{1,0},{2,1},{3,2},{4,3},{5,4},{6,5},{7,6},{8,7},{9,8},{10,9},{11,1... | collective-permute-start | bytes 98312 | tf_op jit(solution)/shard_map/while/body/eval_jaxpr/ppermute | solution.py:18
  890.4 19.4 %collective-permute-start.1 = (f32[1,16,512]{2,1,0:T(8,128)S(1)}, f32[1,16,512]{2,1,0:T(8,128)S(1)}, u32[]{:S(2)}, u32[]{:S(2)}) collective-permute-start(f32[1,16,512]{2,1,0:T(8,128)S(1)} %get-tuple-element.401), channel_id=1, source_target_pairs={{0,1},{1,2},{2,3},{3,4},{4,5},{5,6},{6,7},{7,8},{8,9},{9,10},{10,1... | collective-permute-start | bytes 98312 | tf_op jit(solution)/shard_map/while/body/eval_jaxpr/ppermute | solution.py:17
  929.4 10.5 collective-permute-start.2
  939.9 21.0 %collective-permute-start = (f32[1,16,512]{2,1,0:T(8,128)S(1)}, f32[1,16,512]{2,1,0:T(8,128)S(1)}, u32[]{:S(2)}, u32[]{:S(2)}) collective-permute-start(f32[1,16,512]{2,1,0:T(8,128)S(1)} %get-tuple-element.400), channel_id=1, source_target_pairs={{1,0},{2,1},{3,2},{4,3},{5,4},{6,5},{7,6},{8,7},{9,8},{10,9},{11,1... | collective-permute-start | bytes 98312 | tf_op jit(solution)/shard_map/while/body/eval_jaxpr/ppermute | solution.py:18
  941.8 19.4 %collective-permute-start.1 = (f32[1,16,512]{2,1,0:T(8,128)S(1)}, f32[1,16,512]{2,1,0:T(8,128)S(1)}, u32[]{:S(2)}, u32[]{:S(2)}) collective-permute-start(f32[1,16,512]{2,1,0:T(8,128)S(1)} %get-tuple-element.401), channel_id=1, source_target_pairs={{0,1},{1,2},{2,3},{3,4},{4,5},{5,6},{6,7},{7,8},{8,9},{9,10},{10,1... | collective-permute-start | bytes 98312 | tf_op jit(solution)/shard_map/while/body/eval_jaxpr/ppermute | solution.py:17
  980.9 10.5 collective-permute-start.2
  991.4 21.0 %collective-permute-start = (f32[1,16,512]{2,1,0:T(8,128)S(1)}, f32[1,16,512]{2,1,0:T(8,128)S(1)}, u32[]{:S(2)}, u32[]{:S(2)}) collective-permute-start(f32[1,16,512]{2,1,0:T(8,128)S(1)} %get-tuple-element.400), channel_id=1, source_target_pairs={{1,0},{2,1},{3,2},{4,3},{5,4},{6,5},{7,6},{8,7},{9,8},{10,9},{11,1... | collective-permute-start | bytes 98312 | tf_op jit(solution)/shard_map/while/body/eval_jaxpr/ppermute | solution.py:18
  993.3 19.4 %collective-permute-start.1 = (f32[1,16,512]{2,1,0:T(8,128)S(1)}, f32[1,16,512]{2,1,0:T(8,128)S(1)}, u32[]{:S(2)}, u32[]{:S(2)}) collective-permute-start(f32[1,16,512]{2,1,0:T(8,128)S(1)} %get-tuple-element.401), channel_id=1, source_target_pairs={{0,1},{1,2},{2,3},{3,4},{4,5},{5,6},{6,7},{7,8},{8,9},{9,10},{10,1... | collective-permute-start | bytes 98312 | tf_op jit(solution)/shard_map/while/body/eval_jaxpr/ppermute | solution.py:17
  1032.3 10.5 collective-permute-start.2
  1042.8 19.2 %collective-permute-start.11 = (f32[1,16,512]{2,1,0:T(8,128)S(1)}, f32[1,16,512]{2,1,0:T(8,128)S(1)}, u32[]{:S(2)}, u32[]{:S(2)}) collective-permute-start(f32[1,16,512]{2,1,0:T(8,128)S(1)} %get-tuple-element.245), channel_id=1, source_target_pairs={{0,1},{1,2},{2,3},{3,4},{4,5},{5,6},{6,7},{7,8},{8,9},{9,10},{10,1... | collective-permute-start | bytes 98312 | tf_op jit(solution)/shard_map/ppermute | solution.py:17
  1060.1 18.7 %collective-permute-start.12 = (f32[1,16,512]{2,1,0:T(8,128)S(1)}, f32[1,16,512]{2,1,0:T(8,128)S(1)}, u32[]{:S(2)}, u32[]{:S(2)}) collective-permute-start(f32[1,16,512]{2,1,0:T(8,128)S(1)} %get-tuple-element.246), channel_id=1, source_target_pairs={{1,0},{2,1},{3,2},{4,3},{5,4},{6,5},{7,6},{8,7},{9,8},{10,9},{11,1... | collective-permute-start | bytes 98312 | tf_op jit(solution)/shard_map/ppermute | solution.py:18
where the time goes:
time: 1110 us; the launch traced here: 1100 us
  other arithmetic  400 us (36%)
  starting transfers between devices  400 us (36%)
  waiting for transfers between devices  269 us (24%)
  local copies, waits for them, and re-layouts  28.5 us (3%)
    ppermute x20, starting transfers between devices, extended_2(): before = lax.ppermute(last, axis, up)  331 us
    select_n x15, other arithmetic, relay_round(): jnp.where(slice_index == 0, fine_end, coarse(carried, coarse_kernel) + ju...  288 us
    ppermute x15, waiting for transfers between devices, passed_along(): return lax.ppermute(shard, axis, pairs)  129 us
    ppermute x20, waiting for transfers between devices, extended_2(): before = lax.ppermute(last, axis, up)  108 us
    add x16, other arithmetic, advance(): return values - transport + coef_stack[0] * laplace  54.2 us
    ppermute x20, starting transfers between devices, extended_2(): after = lax.ppermute(leading, axis, down)  40.4 us
    ppermute x20, waiting for transfers between devices, extended_2(): after = lax.ppermute(leading, axis, down)  32.2 us
    ppermute x15, starting transfers between devices, passed_along(): return lax.ppermute(shard, axis, pairs)  28.8 us
  transfers between devices with their start and end apart: 55, of which 34 were waited for; matrix products, arithmetic and copies ran while one was open for 5% of the time, Pallas kernels for 0%

commit v1 on v0

v1 whole, which is shorter than its diff:
```python
import functools

import jax
import jax.numpy as jnp
from jax import lax
from jax.experimental import pallas as pl
from jax.experimental.pallas import tpu as pltpu
from jax.sharding import PartitionSpec as P

FINE = 16
ZONES = 16
ROWS = 16
NZ = 16
NY = 512
TILES = 4
LANES = 128
EXT = ROWS + 2 * FINE
MESH = pl.DeviceIdType.MESH
HIGH = lax.Precision.HIGHEST


def iotas(shape):
    return lax.broadcasted_iota(jnp.int32, shape, 0), lax.broadcasted_iota(jnp.int32, shape, 1)


def shift_down(v):
    return jnp.concatenate([pltpu.roll(v[:, NY - LANES :], 1, 1), v[:, : NY - LANES]], axis=1)


def shift_up(v):
    return jnp.concatenate([v[:, LANES:], pltpu.roll(v[:, :LANES], LANES - 1, 1)], axis=1)


def coarse_row(src, x, ck):
    zi, li = iotas((NZ, LANES))
    sums = [[], [], []]
    for tile in range(TILES):
        part = [None] * 3
        for a in range(3):
            v = src[x + a - 1, :, tile * LANES : (tile + 1) * LANES]
            below = jnp.where(zi == 0, 0.0, pltpu.roll(v, 1, 0))
            above = jnp.where(zi == NZ - 1, 0.0, pltpu.roll(v, NZ - 1, 0))
            for b, w in enumerate((below, v, above)):
                for c in range(3):
                    term = ck[a, b, c] * w
                    part[c] = term if part[c] is None else part[c] + term
        for c in range(3):
            sums[c].append(part[c])
    low = [jnp.where(li == 0, 0.0, pltpu.roll(sums[0][TILES - 1], 1, 1))] + sums[0][:-1]
    high = sums[2][1:] + [jnp.where(li == LANES - 1, 0.0, pltpu.roll(sums[2][0], LANES - 1, 1))]
    return jnp.concatenate([low[j] + sums[1][j] + high[j] for j in range(TILES)], axis=1)


def kernel(
    zv, cond, xv, cv, ck, starts, zmap, out,
    perm, u, zone, w, gs, ja, jb, cin, ca, cb, co,
    halo_send, halo_recv, ja_send, ja_recv, jb_send, jb_recv, c_send, c_recv, a_send, a_recv,
):
    t = lax.axis_index("tm")
    s = lax.axis_index("space")
    slices = lax.axis_size("tm")
    parts = lax.axis_size("space")
    chip = t // 2
    odd = lax.rem(t, 2) == 1
    even = lax.rem(t, 2) == 0
    has_low = s > 0
    has_high = s < parts - 1
    mate = t + 1 - 2 * lax.rem(t, 2)

    def at(tm, space):
        return {"tm": tm, "space": space}

    barrier = pltpu.get_barrier_semaphore()

    def greet(tm, space):
        pl.semaphore_signal(barrier, inc=1, device_id=at(tm, space), device_id_type=MESH)

    @pl.when(has_low)
    def _():
        greet(t, s - 1)

    @pl.when(has_high)
    def _():
        greet(t, s + 1)

    @pl.when(jnp.logical_and(odd, has_low))
    def _():
        greet(t - 1, s - 1)

    @pl.when(jnp.logical_and(odd, has_high))
    def _():
        greet(t - 1, s + 1)

    greet(mate, s)

    @pl.when(jnp.logical_and(odd, t >= 3))
    def _():
        greet(t - 2, s)

    yi, pi = iotas((NY, NY))
    perm[...] = jnp.where(yi == TILES * lax.rem(pi, LANES) + pi // LANES, 1.0, 0.0)
    own = starts[0].reshape(ROWS * NZ, NY)
    u[0, FINE : FINE + ROWS] = jnp.dot(
        own, perm[...], precision=HIGH, preferred_element_type=jnp.float32
    ).reshape(ROWS, NZ, NY)
    zone[FINE : FINE + ROWS] = jnp.dot(
        zmap[...].reshape(ROWS * NZ, NY).astype(jnp.float32),
        perm[...],
        preferred_element_type=jnp.float32,
    ).reshape(ROWS, NZ, NY)

    zero_row = jnp.zeros((NZ, NY), jnp.float32)

    @pl.when(jnp.logical_not(has_low))
    def _():
        for buf in (u.at[0], u.at[1], cin, ca):
            buf[FINE - 1] = zero_row

    @pl.when(jnp.logical_not(has_high))
    def _():
        for buf in (u.at[0], u.at[1], cin, ca):
            buf[FINE + ROWS] = zero_row

    low_count = has_low.astype(jnp.int32)
    high_count = has_high.astype(jnp.int32)
    near = low_count + high_count
    pl.semaphore_wait(
        barrier,
        near
        + jnp.where(even, near, 0)
        + 1
        + jnp.where(jnp.logical_and(odd, t < slices - 1), 1, 0),
    )

    def halo(kind, up):
        buf = u.at[0] if kind == 0 else zone
        n = 2 * kind + up
        return pltpu.make_async_remote_copy(
            src_ref=buf.at[pl.ds(FINE, ROWS)],
            dst_ref=buf.at[pl.ds(0 if up else FINE + ROWS, ROWS)],
            send_sem=halo_send.at[n],
            recv_sem=halo_recv.at[n],
            device_id=at(t, s + 1 if up else s - 1),
            device_id_type=MESH,
        )

    for kind in (1, 0):

        @pl.when(has_high)
        def _():
            halo(kind, 1).start()

        @pl.when(has_low)
        def _():
            halo(kind, 0).start()

    numbers = []
    for q in range(ZONES):
        v = zv[q]
        numbers.append((cond[q], xv[v], cv[1, v], cv[0, v]))
    zi, li = iotas((NZ, LANES))

    def weights(x, carry):
        for tile in range(TILES):
            sl = slice(tile * LANES, (tile + 1) * LANES)
            z = zone[x, :, sl].astype(jnp.int32)
            bits = [(z & (1 << b)) != 0 for b in range(4)]
            found = []
            for n in range(4):
                level = [numbers[q][n] for q in range(ZONES)]
                for b in range(4):
                    level = [
                        jnp.where(bits[b], level[2 * j + 1], level[2 * j])
                        for j in range(len(level) // 2)
                    ]
                found.append(level[0])
            d, cx, cz, cy = found
            xm = d + jnp.maximum(cx, 0.0)
            xp = d - jnp.minimum(cx, 0.0)
            zm = d + jnp.maximum(cz, 0.0)
            zp = d - jnp.minimum(cz, 0.0)
            ym = d + jnp.maximum(cy, 0.0)
            yp = d - jnp.minimum(cy, 0.0)
            w[0, x, :, sl] = 1.0 - (((xm + xp) + (zm + zp)) + (ym + yp))
            w[1, x, :, sl] = xm
            w[2, x, :, sl] = xp
            w[3, x, :, sl] = jnp.where(zi == 0, 0.0, zm)
            w[4, x, :, sl] = jnp.where(zi == NZ - 1, 0.0, zp)
            if tile == 0:
                ym = jnp.where(li == 0, 0.0, ym)
            if tile == TILES - 1:
                yp = jnp.where(li == LANES - 1, 0.0, yp)
            w[5, x, :, sl] = ym
            w[6, x, :, sl] = yp
        return carry

    lax.fori_loop(FINE, FINE + ROWS, weights, 0)

    def start_coarse(x, carry):
        gs[x - FINE] = coarse_row(u.at[0], x, ck)
        return carry

    lax.fori_loop(FINE + 1, FINE + ROWS - 1, start_coarse, 0)

    @pl.when(has_low)
    def _():
        halo(1, 1).wait_recv()
        halo(0, 1).wait_recv()
        lax.fori_loop(0, FINE, weights, 0)

    @pl.when(has_high)
    def _():
        halo(1, 0).wait_recv()
        halo(0, 0).wait_recv()
        lax.fori_loop(FINE + ROWS, EXT, weights, 0)

    @pl.when(has_low)
    def _():
        halo(1, 0).wait_send()
        halo(0, 0).wait_send()

    @pl.when(has_high)
    def _():
        halo(1, 1).wait_send()
        halo(0, 1).wait_send()

    start_coarse(FINE, 0)
    start_coarse(FINE + ROWS - 1, 0)

    first_row = jnp.where(has_low, 0, FINE)
    end_row = jnp.where(has_high, EXT, FINE + ROWS)

    def step(level, src, dst):
        lo = jnp.maximum(level, first_row)
        hi = jnp.minimum(EXT - level, end_row)

        def row(x, carry):
            v = src[x]
            acc = w[0, x] * v
            acc += w[1, x] * src[x - 1]
            acc += w[2, x] * src[x + 1]
            acc += w[3, x] * pltpu.roll(v, 1, 0)
            acc += w[4, x] * pltpu.roll(v, NZ - 1, 0)
            acc += w[5, x] * shift_down(v)
            acc += w[6, x] * shift_up(v)
            dst[x] = acc
            return carry

        lax.fori_loop(lo, hi, row, 0)

    def two_steps(n, carry):
        step(2 * n + 1, u.at[0], u.at[1])
        step(2 * n + 2, u.at[1], u.at[0])
        return carry

    lax.fori_loop(0, FINE // 2, two_steps, 0)

    keep = jnp.where(t == 0, 0.0, 1.0).astype(jnp.float32)
    depth = slices - 1 - 2 * chip

    def j_copy(x, to_low, to_high, on_even):
        buf = ja if on_even else jb
        send, recv = (ja_send, ja_recv) if on_even else (jb_send, jb_recv)
        space = s - 1 if to_low else (s + 1 if to_high else s)
        to = x + ROWS if to_low else (x - ROWS if to_high else x)
        return pltpu.make_async_remote_copy(
            src_ref=buf.at[FINE + x],
            dst_ref=buf.at[FINE + to],
            send_sem=send.at[0 if to_low else (1 if to_high else 2), x],
            recv_sem=recv.at[FINE + to],
            device_id=at(t + 1 if on_even else t, space),
            device_id_type=MESH,
        )

    def each_jump_copy(x, act):
        @pl.when(even)
        def _():
            @pl.when(jnp.logical_and(has_high, x >= ROWS - depth))
            def _():
                act(j_copy(x, False, True, True))

            @pl.when(jnp.logical_and(has_low, x < depth))
            def _():
                act(j_copy(x, True, False, True))

            act(j_copy(x, False, False, True))

        @pl.when(odd)
        def _():
            @pl.when(jnp.logical_and(has_high, x > ROWS - depth))
            def _():
                act(j_copy(x, False, True, False))

            @pl.when(jnp.logical_and(has_low, x < depth - 1))
            def _():
                act(j_copy(x, True, False, False))

    def make_jump(x, carry):
        value = u[0, FINE + x] - keep * gs[x]

        @pl.when(even)
        def _():
            ja[FINE + x] = value

        @pl.when(odd)
        def _():
            jb[FINE + x] = value

        each_jump_copy(x, lambda copy: copy.start())
        return carry

    lax.fori_loop(0, ROWS, make_jump, 0)

    low_end = jnp.where(has_low, -FINE, 0)
    high_end = jnp.where(has_high, ROWS + FINE - 1, ROWS - 1)
    lo_a = jnp.maximum(-depth, low_end)
    hi_a = jnp.minimum(ROWS - 1 + depth, high_end)
    lo_b = jnp.maximum(1 - depth, low_end)
    hi_b = jnp.minimum(ROWS - 2 + depth, high_end)
    lo_i = jnp.maximum(-depth - 1, low_end)
    hi_i = jnp.minimum(ROWS + depth, high_end)
    passes_on = t < slices - 1

    def c_copy(x):
        return pltpu.make_async_remote_copy(
            src_ref=cb.at[FINE + x],
            dst_ref=cin.at[FINE + x],
            send_sem=c_send.at[FINE + x],
            recv_sem=c_recv.at[FINE + x],
            device_id=at(t + 2, s),
            device_id_type=MESH,
        )

    def a_copy(x):
        return pltpu.make_async_remote_copy(
            src_ref=ca.at[FINE + x],
            dst_ref=co.at[x],
            send_sem=a_send.at[x],
            recv_sem=a_recv.at[x],
            device_id=at(mate, s),
            device_id_type=MESH,
        )

    def j_wait(x, on_even):
        buf, recv = (ja, ja_recv) if on_even else (jb, jb_recv)
        pltpu.make_async_remote_copy(
            src_ref=buf.at[FINE + x],
            dst_ref=buf.at[FINE + x],
            send_sem=(ja_send if on_even else jb_send).at[0, 0],
            recv_sem=recv.at[FINE + x],
            device_id=at(t, s),
            device_id_type=MESH,
        ).wait_recv()

    @pl.when(odd)
    def _():
        @pl.when(chip > 0)
        def _():
            def wait_in(x, carry):
                c_copy(x).wait_recv()
                return carry

            lax.fori_loop(lo_i, lo_a + 1, wait_in, 0)

        def relay(x, carry):
            @pl.when(jnp.logical_and(chip > 0, x + 1 <= hi_i))
            def _():
                c_copy(x + 1).wait_recv()

            @pl.when(x <= hi_a)
            def _():
                j_wait(x, True)

                @pl.when(chip == 0)
                def _():
                    ca[FINE + x] = ja[FINE + x]

                @pl.when(chip > 0)
                def _():
                    ca[FINE + x] = coarse_row(cin, FINE + x, ck) + ja[FINE + x]

            @pl.when(jnp.logical_and(x >= 0, x < ROWS))
            def _():
                a_copy(x).start()

            y = x - 1

            @pl.when(jnp.logical_and(y >= lo_b, y <= hi_b))
            def _():
                @pl.when(jnp.logical_or(y < 0, y >= ROWS))
                def _():
                    j_wait(y, False)

                cb[FINE + y] = coarse_row(ca, FINE + y, ck) + jb[FINE + y]

                @pl.when(passes_on)
                def _():
                    c_copy(y).start()

            return carry

        lax.fori_loop(lo_a, hi_b + 2, relay, 0)
        co[...] = cb[FINE : FINE + ROWS]

    @pl.when(even)
    def _():
        def wait_a(x, carry):
            a_copy(x).wait_recv()
            return carry

        lax.fori_loop(0, ROWS, wait_a, 0)

    out[...] = lax.dot_general(
        co[...].reshape(ROWS * NZ, NY),
        perm[...],
        (((1,), (1,)), ((), ())),
        precision=HIGH,
        preferred_element_type=jnp.float32,
    ).reshape(1, ROWS, NZ, NY)

    def drain_jump(x, carry):
        each_jump_copy(x, lambda copy: copy.wait_send())

        @pl.when(odd)
        def _():
            a_copy(x).wait_send()

        return carry

    lax.fori_loop(0, ROWS, drain_jump, 0)

    @pl.when(jnp.logical_and(odd, passes_on))
    def _():
        def drain(x, carry):
            c_copy(x).wait_send()
            return carry

        lax.fori_loop(lo_b, hi_b + 1, drain, 0)


def shards(
    starts, zone_map, zone_velocity, conductivity, x_velocity, cross_velocity, coarse_kernel
):
    smem = pl.BlockSpec(memory_space=pltpu.SMEM)
    vmem = pl.BlockSpec(memory_space=pltpu.VMEM)
    field = lambda rows: pltpu.VMEM((rows, NZ, NY), jnp.float32)
    dma = pltpu.SemaphoreType.DMA
    return pl.pallas_call(
        kernel,
        name="parareal",
        out_shape=jax.ShapeDtypeStruct(starts.shape, jnp.float32),
        in_specs=[smem] * 5 + [vmem] * 2,
        out_specs=vmem,
        scratch_shapes=[
            pltpu.VMEM((NY, NY), jnp.float32),
            pltpu.VMEM((2, EXT, NZ, NY), jnp.float32),
            field(EXT),
            pltpu.VMEM((7, EXT, NZ, NY), jnp.float32),
            field(ROWS),
            field(EXT),
            field(EXT),
            field(EXT),
            field(EXT),
            field(EXT),
            field(ROWS),
            dma((4,)),
            dma((4,)),
            dma((3, ROWS)),
            dma((EXT,)),
            dma((3, ROWS)),
            dma((EXT,)),
            dma((EXT,)),
            dma((EXT,)),
            dma((ROWS,)),
            dma((ROWS,)),
        ],
        compiler_params=pltpu.CompilerParams(
            collective_id=0, has_side_effects=True, vmem_limit_bytes=56 * 2**20
        ),
    )(
        zone_velocity, conductivity, x_velocity, cross_velocity, coarse_kernel, starts, zone_map
    )


def solution(mesh):
    in_specs = (P("tm", "space", None, None), P("space", None, None), P(), P(), P(), P(), P())
    out_specs = P("tm", "space", None, None)
    return jax.shard_map(shards, mesh=mesh, in_specs=in_specs, out_specs=out_specs, check_vma=False)
```

time: 1110 us -> 189 us (0.17)
  the two profiles are of different devices: /device:TPU:62 before, /device:TPU:481 now
where the time goes in v1:
time: 189 us
  Pallas kernels  187 us (99%)
    pallas_call x1, Pallas kernels, shards(): pl.pallas_call(kernel, name='parareal', out_shape=jax.ShapeDtypeStruct(st...  187 us

profile of v1, /device:TPU:481, one launch (start us, length us, event | category | flops | bytes accessed | tf_op | source)
XLA Modules:
  0.0 189.3 jit_solution(8861900610703044416)
XLA Ops:
  0.0 187.4 %parareal.1 = f32[1,16,16,512]{3,2,1,0:T(8,128)} custom-call(s32[16]{0:T(128)} %zv.1, f32[16]{0:T(128)} %cond.1, f32[16]{0:T(128)} %xv.1, f32[2,16]{1,0:T(2,128)} %cv.1, f32[3,3,3]{2,1,0:T(4,128)} %ck.1, f32[1,16,16,512]{3,2,1,0:T(8,128)} %starts.1, s32[16,16,512]{2,1,0:T(8,128)} %zmap.1), custom_call_target="tpu_custom_call" | custom-call | tf_op jit(solution)/shard_map/parareal/pallas_call | solution.py:448
  187.4 1.9 copy.9

commit v2 on v1

v2 whole, which is shorter than its diff:
```python
import functools

import jax
import jax.numpy as jnp
from jax import lax
from jax.experimental import pallas as pl
from jax.experimental.pallas import tpu as pltpu
from jax.sharding import PartitionSpec as P

FINE = 16
ZONES = 16
ROWS = 16
NZ = 16
NY = 512
TILES = 4
LANES = 128
EXT = ROWS + 2 * FINE
BLOCK = 8
PAD = 24
WIDE = ROWS + 2 * PAD
MESH = pl.DeviceIdType.MESH
HIGH = lax.Precision.HIGHEST


def iotas(shape):
    return lax.broadcasted_iota(jnp.int32, shape, 0), lax.broadcasted_iota(jnp.int32, shape, 1)


def shift_down(v):
    return jnp.concatenate([pltpu.roll(v[:, NY - LANES :], 1, 1), v[:, : NY - LANES]], axis=1)


def shift_up(v):
    return jnp.concatenate([v[:, LANES:], pltpu.roll(v[:, :LANES], LANES - 1, 1)], axis=1)


def coarse_row(src, x, ck):
    zi, li = iotas((NZ, LANES))
    sums = [[], [], []]
    for tile in range(TILES):
        part = [None] * 3
        for a in range(3):
            v = src[x + a - 1, :, tile * LANES : (tile + 1) * LANES]
            below = jnp.where(zi == 0, 0.0, pltpu.roll(v, 1, 0))
            above = jnp.where(zi == NZ - 1, 0.0, pltpu.roll(v, NZ - 1, 0))
            for b, w in enumerate((below, v, above)):
                for c in range(3):
                    term = ck[a, b, c] * w
                    part[c] = term if part[c] is None else part[c] + term
        for c in range(3):
            sums[c].append(part[c])
    low = [jnp.where(li == 0, 0.0, pltpu.roll(sums[0][TILES - 1], 1, 1))] + sums[0][:-1]
    high = sums[2][1:] + [jnp.where(li == LANES - 1, 0.0, pltpu.roll(sums[2][0], LANES - 1, 1))]
    return jnp.concatenate([low[j] + sums[1][j] + high[j] for j in range(TILES)], axis=1)


def kernel(
    zv, cond, xv, cv, ck, starts, zmap, out,
    perm, u, first, zone, w, gs, ja, jb, cin, ca, cb, co, rbuf,
    u_send, u_recv, z_send, z_recv, zm_send, zm_recv, zf_send, r_send, r_recv, f_send,
    ja_send, ja_recv, jb_send, jb_recv, jm_send, jm_recv, c_send, c_recv, a_send, a_recv,
):
    t = lax.axis_index("tm")
    s = lax.axis_index("space")
    slices = lax.axis_size("tm")
    parts = lax.axis_size("space")
    chips = slices // 2
    chip = t // 2
    core = lax.rem(t, 2)
    odd = core == 1
    even = core == 0
    has_low = s > 0
    has_high = s < parts - 1
    mate = t + 1 - 2 * core
    half = parts // 2
    far_low = s == half
    far_high = s == half - 1
    far = jnp.logical_or(far_low, far_high)
    over = jnp.where(far_low, s - 1, s + 1)
    ascending = s < half
    end_chip = jnp.logical_or(chip == 0, chip == chips - 1)
    seeds = jnp.logical_and(far, end_chip)
    across = 2 * (chips - 1 - chip) + core
    goes_on = jnp.logical_and(
        far, jnp.logical_and(chip != chips // 2 - 1, chip != chips // 2)
    )
    next_t = jnp.where(chip < chips // 2, t + 2, t - 2)
    last_t = jnp.where(chip < chips // 2, t - 2, t + 2)
    low_helper = [s == half - 5, s == half - 13]
    high_helper = [s == half + 4, s == half + 12]
    helps_up = jnp.logical_or(low_helper[0], low_helper[1])
    helps_down = jnp.logical_or(high_helper[0], high_helper[1])
    helps = jnp.logical_or(helps_up, helps_down)

    def at(tm, space):
        return {"tm": tm, "space": space}

    def both(a, b):
        return jnp.logical_and(a, b)

    def remote(src, dst, send, recv, device):
        return pltpu.make_async_remote_copy(
            src_ref=src,
            dst_ref=dst,
            send_sem=send,
            recv_sem=recv,
            device_id=device,
            device_id_type=MESH,
        )

    barrier = pltpu.get_barrier_semaphore()

    def greet(tm, space):
        pl.semaphore_signal(barrier, inc=1, device_id=at(tm, space), device_id_type=MESH)

    @pl.when(far)
    def _():
        greet(t, jnp.where(far_low, half - 5, half + 4))
        greet(t, jnp.where(far_low, half - 13, half + 12))

        @pl.when(end_chip)
        def _():
            greet(across, over)

        @pl.when(jnp.logical_not(end_chip))
        def _():
            greet(last_t, s)

    @pl.when(helps)
    def _():
        greet(t, jnp.where(helps_up, half - 1, half))

    @pl.when(has_low)
    def _():
        greet(t, s - 1)

    @pl.when(has_high)
    def _():
        greet(t, s + 1)

    @pl.when(both(odd, has_low))
    def _():
        greet(t - 1, s - 1)

    @pl.when(both(odd, has_high))
    def _():
        greet(t - 1, s + 1)

    greet(mate, s)

    @pl.when(both(odd, t >= 3))
    def _():
        greet(t - 2, s)

    yi, pi = iotas((NY, NY))
    perm[...] = jnp.where(yi == TILES * lax.rem(pi, LANES) + pi // LANES, 1.0, 0.0)
    own = starts[0].reshape(ROWS * NZ, NY)
    zone[FINE : FINE + ROWS] = jnp.dot(
        zmap[...].reshape(ROWS * NZ, NY).astype(jnp.float32),
        perm[...],
        preferred_element_type=jnp.float32,
    ).reshape(ROWS, NZ, NY)
    initial = jnp.dot(
        own, perm[...], precision=HIGH, preferred_element_type=jnp.float32
    ).reshape(ROWS, NZ, NY)
    u[0, PAD : PAD + ROWS] = initial
    first[...] = initial

    zero_row = jnp.zeros((NZ, NY), jnp.float32)

    def clear(begin, edge):
        cin[edge] = zero_row
        ca[edge] = zero_row

        def row(x, carry):
            u[0, x] = zero_row
            u[1, x] = zero_row
            for n in range(7):
                w[n, x] = zero_row
            return carry

        lax.fori_loop(begin, begin + PAD - 4, row, 0)

    @pl.when(jnp.logical_not(has_low))
    def _():
        clear(4, FINE - 1)

    @pl.when(jnp.logical_not(has_high))
    def _():
        clear(PAD + ROWS, FINE + ROWS)

    def count(flag):
        return flag.astype(jnp.int32)

    near = count(has_low) + count(has_high)
    pl.semaphore_wait(
        barrier,
        near
        + jnp.where(even, near, 0)
        + 1
        + count(both(odd, t < slices - 1))
        + count(seeds)
        + count(goes_on)
        + 2 * count(far)
        + count(helps),
    )

    def z_half(side, c):
        at_row = FINE - BLOCK - BLOCK * c if side == 0 else FINE + ROWS + BLOCK * c
        return zone.at[pl.ds(at_row, BLOCK)]

    def z_copy(side, tm, space):
        source = FINE + BLOCK - BLOCK * core if side == 0 else FINE + BLOCK * core
        return remote(
            zone.at[pl.ds(source, BLOCK)],
            z_half(side, core),
            z_send.at[side],
            z_recv.at[side],
            at(tm, space),
        )

    def z_mate(side):
        return remote(
            z_half(side, core), z_half(side, core), zm_send.at[side], zm_recv.at[side], at(mate, s)
        )

    def z_mate_wait(side):
        part = z_half(side, 1 - core)
        remote(part, part, zm_send.at[side], zm_recv.at[side], at(mate, s)).wait_recv()

    def z_next(side):
        part = z_half(side, core)
        return remote(part, part, zf_send, z_recv.at[side], at(next_t, s))

    def each_zone_copy(act):
        @pl.when(both(has_high, jnp.logical_not(far_high)))
        def _():
            act(z_copy(0, t, s + 1))

        @pl.when(both(has_low, jnp.logical_not(far_low)))
        def _():
            act(z_copy(1, t, s - 1))

        @pl.when(both(far_high, end_chip))
        def _():
            act(z_copy(0, across, s + 1))

        @pl.when(both(far_low, end_chip))
        def _():
            act(z_copy(1, across, s - 1))

    def u_rows(start_row, rows):
        return u.at[0, pl.ds(PAD + start_row, rows)]

    def u_copy(side, batch):
        if side == 0:
            source, to, space = BLOCK - BLOCK * batch, -BLOCK - BLOCK * batch, s + 1
        else:
            source, to, space = BLOCK * batch, ROWS + BLOCK * batch, s - 1
        return remote(
            first.at[pl.ds(source, BLOCK)],
            u_rows(to, BLOCK),
            u_send.at[side, batch],
            u_recv.at[side, batch],
            at(t, space),
        )

    pieces = ((0, 0, 4, -1), (0, 4, 2, 0), (0, 6, 2, 1), (1, 8, 2, -1), (1, 10, 3, 0), (1, 13, 3, 1))

    def piece_copy(side, number):
        batch, skip, rows, helper = pieces[number]
        source = ROWS - skip - rows if side == 0 else skip
        to = -skip - rows if side == 0 else ROWS + skip
        if helper < 0:
            dst, recv, space = u_rows(to, rows), u_recv.at[side, batch], half if side == 0 else half - 1
        else:
            dst, recv = rbuf.at[pl.ds(2 * batch, rows)], r_recv.at[batch]
            space = (
                (half - 5, half - 13)[helper] if side == 0 else (half + 4, half + 12)[helper]
            )
        return remote(first.at[pl.ds(source, rows)], dst, r_send.at[number], recv, at(t, space))

    def forward_copy(side, number):
        batch, skip, rows, helper = pieces[number]
        to = -skip - rows if side == 0 else ROWS + skip
        return remote(
            rbuf.at[pl.ds(2 * batch, rows)],
            u_rows(to, rows),
            f_send.at[batch],
            u_recv.at[side, batch],
            at(t, half if side == 0 else half - 1),
        )

    def each_piece(act):
        for side, flag in ((0, far_high), (1, far_low)):

            @pl.when(flag)
            def _():
                for number in (1, 2, 0, 4, 5, 3):
                    act(piece_copy(side, number))

    def each_forward(act):
        for side, flags in ((0, low_helper), (1, high_helper)):
            for helper in range(2):

                @pl.when(flags[helper])
                def _():
                    for number in range(len(pieces)):
                        if pieces[number][3] == helper:
                            act(side, number)

    def each_state_copy(batch, act):
        @pl.when(both(has_high, jnp.logical_not(far_high)))
        def _():
            act(u_copy(0, batch))

        @pl.when(both(has_low, jnp.logical_not(far_low)))
        def _():
            act(u_copy(1, batch))

    start = lambda copy: copy.start()
    sent = lambda copy: copy.wait_send()
    each_zone_copy(start)
    each_piece(start)
    each_state_copy(0, start)
    each_state_copy(1, start)

    numbers = []
    for q in range(ZONES):
        v = zv[q]
        numbers.append((cond[q], xv[v], cv[1, v], cv[0, v]))
    zi, li = iotas((NZ, LANES))

    def weights(x, carry):
        for tile in range(TILES):
            sl = slice(tile * LANES, (tile + 1) * LANES)
            z = zone[FINE + x, :, sl].astype(jnp.int32)
            bits = [(z & (1 << b)) != 0 for b in range(4)]
            found = []
            for n in range(4):
                level = [numbers[q][n] for q in range(ZONES)]
                for b in range(4):
                    level = [
                        jnp.where(bits[b], level[2 * j + 1], level[2 * j])
                        for j in range(len(level) // 2)
                    ]
                found.append(level[0])
            d, cx, cz, cy = found
            xm = d + jnp.maximum(cx, 0.0)
            xp = d - jnp.minimum(cx, 0.0)
            zm = d + jnp.maximum(cz, 0.0)
            zp = d - jnp.minimum(cz, 0.0)
            ym = d + jnp.maximum(cy, 0.0)
            yp = d - jnp.minimum(cy, 0.0)
            w[0, PAD + x, :, sl] = 1.0 - (((xm + xp) + (zm + zp)) + (ym + yp))
            w[1, PAD + x, :, sl] = xm
            w[2, PAD + x, :, sl] = xp
            w[3, PAD + x, :, sl] = jnp.where(zi == 0, 0.0, zm)
            w[4, PAD + x, :, sl] = jnp.where(zi == NZ - 1, 0.0, zp)
            if tile == 0:
                ym = jnp.where(li == 0, 0.0, ym)
            if tile == TILES - 1:
                yp = jnp.where(li == LANES - 1, 0.0, yp)
            w[5, PAD + x, :, sl] = ym
            w[6, PAD + x, :, sl] = yp
        return carry

    lax.fori_loop(0, ROWS, weights, 0)

    def start_coarse(x):
        gs[x] = coarse_row(u.at[0], PAD + x, ck)

    def two_coarse(n, carry):
        start_coarse(2 * n + 1)
        start_coarse(2 * n + 2)
        return carry

    lax.fori_loop(0, ROWS // 2 - 1, two_coarse, 0)

    def forward(side, number):
        piece_copy(side, number).wait_recv()
        forward_copy(side, number).start()

    each_forward(forward)

    for side, flag, is_far in ((0, has_low, far_low), (1, has_high, far_high)):

        @pl.when(flag)
        def _():
            z_copy(side, t, s).wait_recv()
            z_mate(side).start()

            @pl.when(both(is_far, goes_on))
            def _():
                z_next(side).start()

    for side, flag in ((0, has_low), (1, has_high)):

        @pl.when(flag)
        def _():
            z_mate_wait(side)
            lax.fori_loop(-FINE if side == 0 else ROWS, 0 if side == 0 else ROWS + FINE, weights, 0)

    def state_wait(side, batch):
        u_copy(side, batch).wait_recv()

    @pl.when(both(ascending, has_low))
    def _():
        state_wait(0, 0)
        state_wait(0, 1)

    @pl.when(both(jnp.logical_not(ascending), has_high))
    def _():
        state_wait(1, 0)
        state_wait(1, 1)

    @pl.when(ascending)
    def _():
        start_coarse(0)

    @pl.when(jnp.logical_not(ascending))
    def _():
        start_coarse(ROWS - 1)

    def block(src, dst, x0):
        base = PAD + jnp.where(ascending, x0, ROWS - BLOCK - x0)
        rows = [
            [src[base + r - 1, :, j * LANES : (j + 1) * LANES] for j in range(TILES)]
            for r in range(BLOCK + 2)
        ]
        for r in range(BLOCK):
            x = base + r
            v = rows[r + 1]
            low = [pltpu.roll(v[TILES - 1], 1, 1)] + v[:-1]
            high = v[1:] + [pltpu.roll(v[0], LANES - 1, 1)]
            for j in range(TILES):
                sl = slice(j * LANES, (j + 1) * LANES)
                centre = w[0, x, :, sl] * v[j]
                along_x = w[1, x, :, sl] * rows[r][j] + w[2, x, :, sl] * rows[r + 2][j]
                along_y = w[5, x, :, sl] * low[j] + w[6, x, :, sl] * high[j]
                along_z = w[3, x, :, sl] * pltpu.roll(v[j], 1, 0) + w[4, x, :, sl] * pltpu.roll(
                    v[j], NZ - 1, 0
                )
                dst[x, :, sl] = (centre + along_x) + (along_y + along_z)

    def wedge(n, carry):
        for src, dst, level in ((u.at[0], u.at[1], 2 * n + 1), (u.at[1], u.at[0], 2 * n + 2)):

            def blocks(m, c):
                block(src, dst, ROWS - level - BLOCK * m)
                return c

            lax.fori_loop(1, (2 * (FINE - level) + 7) // BLOCK + 1, blocks, 0)
        return carry

    lax.fori_loop(0, FINE // 2, wedge, 0)

    def slab(x0):
        def pair(n, carry):
            block(u.at[0], u.at[1], x0 - 2 * n - 1)
            block(u.at[1], u.at[0], x0 - 2 * n - 2)
            return carry

        lax.fori_loop(0, FINE // 2, pair, 0)

    @pl.when(ascending)
    def _():
        state_wait(1, 0)
        start_coarse(ROWS - 1)

    @pl.when(jnp.logical_not(ascending))
    def _():
        state_wait(0, 0)
        start_coarse(0)

    slab(ROWS)

    @pl.when(ascending)
    def _():
        state_wait(1, 1)

    @pl.when(jnp.logical_not(ascending))
    def _():
        state_wait(0, 1)

    slab(ROWS + BLOCK)

    keep = jnp.where(t == 0, 0.0, 1.0).astype(jnp.float32)
    depth = slices - 1 - 2 * chip

    def jump(x):
        return u[0, PAD + x] - keep * gs[x]

    def jump_loop(buf):
        def row(x, carry):
            buf[FINE + x] = jump(x)
            return carry

        lax.fori_loop(0, ROWS, row, 0)

    @pl.when(even)
    def _():
        jump_loop(ja)

    @pl.when(odd)
    def _():
        jump_loop(jb)

    def j_mate():
        part = ja.at[pl.ds(FINE, ROWS)]
        return remote(part, part, jm_send, jm_recv, at(mate, s))

    def j_copy(x, up, on_even):
        buf = ja if on_even else jb
        send, recv = (ja_send, ja_recv) if on_even else (jb_send, jb_recv)
        to = FINE + (x - ROWS if up else x + ROWS)
        return remote(
            buf.at[FINE + x],
            buf.at[to],
            send.at[1 if up else 0, x],
            recv.at[to],
            at(t + 1 if on_even else t, s + 1 if up else s - 1),
        )

    def each_jump_copy(act):
        for on_even, flag, rows in ((True, even, depth), (False, odd, depth - 1)):

            @pl.when(flag)
            def _():
                def row(n, carry):
                    @pl.when(has_high)
                    def _():
                        act(j_copy(ROWS - 1 - n, True, on_even))

                    @pl.when(has_low)
                    def _():
                        act(j_copy(n, False, on_even))

                    return carry

                lax.fori_loop(0, rows, row, 0)

    @pl.when(even)
    def _():
        j_mate().start()

    each_jump_copy(start)

    low_end = jnp.where(has_low, -FINE, 0)
    high_end = jnp.where(has_high, ROWS + FINE - 1, ROWS - 1)
    lo_a = jnp.maximum(-depth, low_end)
    hi_a = jnp.minimum(ROWS - 1 + depth, high_end)
    lo_b = jnp.maximum(1 - depth, low_end)
    hi_b = jnp.minimum(ROWS - 2 + depth, high_end)
    lo_i = jnp.maximum(-depth - 1, low_end)
    hi_i = jnp.minimum(ROWS + depth, high_end)
    passes_on = t < slices - 1
    split = jnp.where(far_high, ROWS - 2 * chip, jnp.where(far_low, 2 * chip, ROWS // 2))
    up_late = jnp.where(far_high, split - lo_a + 1, 0)
    down_late = jnp.where(far_low, hi_a - split + 2, 0)
    up_from = jnp.where(far_high, 0, jnp.where(far_low, 2, 1))
    down_from = jnp.where(far_low, 0, jnp.where(far_high, 2, 1))
    up_steps = up_late + jnp.maximum(hi_a - split, hi_b + 1 - split) + 1
    down_steps = down_late + jnp.maximum(split - 1 - lo_a, split - lo_b) + 1

    def c_copy(x):
        return remote(
            cb.at[FINE + x],
            cin.at[FINE + x],
            c_send.at[FINE + x],
            c_recv.at[FINE + x],
            at(t + 2, s),
        )

    def a_copy(x):
        return remote(ca.at[FINE + x], co.at[x], a_send.at[x], a_recv.at[x], at(mate, s))

    def j_wait(x, on_even):
        buf, recv = (ja, ja_recv) if on_even else (jb, jb_recv)
        remote(
            buf.at[FINE + x],
            buf.at[FINE + x],
            (ja_send if on_even else jb_send).at[0, 0],
            recv.at[FINE + x],
            at(t, s),
        ).wait_recv()

    def within(x, lo, hi):
        return both(x >= lo, x <= hi)

    def outside(x):
        return jnp.logical_or(x < 0, x >= ROWS)

    def in_wait(x):
        @pl.when(both(chip > 0, within(x, lo_i, hi_i)))
        def _():
            c_copy(x).wait_recv()

    def a_row(x):
        @pl.when(outside(x))
        def _():
            j_wait(x, True)

        @pl.when(chip == 0)
        def _():
            ca[FINE + x] = ja[FINE + x]

        @pl.when(chip > 0)
        def _():
            ca[FINE + x] = coarse_row(cin, FINE + x, ck) + ja[FINE + x]

        @pl.when(jnp.logical_not(outside(x)))
        def _():
            a_copy(x).start()

    def b_row(x):
        @pl.when(outside(x))
        def _():
            j_wait(x, False)

        cb[FINE + x] = coarse_row(ca, FINE + x, ck) + jb[FINE + x]

        @pl.when(passes_on)
        def _():
            c_copy(x).start()

    @pl.when(odd)
    def _():
        jm_wait = ja.at[pl.ds(FINE, ROWS)]
        remote(jm_wait, jm_wait, jm_send, jm_recv, at(mate, s)).wait_recv()
        in_wait(split - 1)
        in_wait(split)

        def relay(k, carry):
            up = k - up_late
            down = k - down_late

            @pl.when(both(up >= 0, within(split + up, lo_a, hi_a)))
            def _():
                in_wait(split + up + 1)
                a_row(split + up)

            @pl.when(both(down >= 0, within(split - 1 - down, lo_a, hi_a)))
            def _():
                in_wait(split - 2 - down)
                a_row(split - 1 - down)

            @pl.when(both(up >= up_from, within(split + up - 1, lo_b, hi_b)))
            def _():
                b_row(split + up - 1)

            @pl.when(both(down >= down_from, within(split - down, lo_b, hi_b)))
            def _():
                b_row(split - down)

            return carry

        lax.fori_loop(0, jnp.maximum(up_steps, down_steps), relay, 0)
        co[...] = cb[FINE : FINE + ROWS]

    @pl.when(even)
    def _():
        def wait_a(x, carry):
            a_copy(x).wait_recv()
            return carry

        lax.fori_loop(0, ROWS, wait_a, 0)

    out[...] = lax.dot_general(
        co[...].reshape(ROWS * NZ, NY),
        perm[...],
        (((1,), (1,)), ((), ())),
        precision=HIGH,
        preferred_element_type=jnp.float32,
    ).reshape(1, ROWS, NZ, NY)

    each_zone_copy(sent)
    each_piece(sent)
    each_state_copy(0, sent)
    each_state_copy(1, sent)
    each_forward(lambda side, number: forward_copy(side, number).wait_send())
    for side, flag, is_far in ((0, has_low, far_low), (1, has_high, far_high)):

        @pl.when(flag)
        def _():
            z_mate(side).wait_send()

            @pl.when(both(is_far, goes_on))
            def _():
                z_next(side).wait_send()

    each_jump_copy(sent)

    @pl.when(even)
    def _():
        j_mate().wait_send()

    @pl.when(odd)
    def _():
        def drain_a(x, carry):
            a_copy(x).wait_send()
            return carry

        lax.fori_loop(0, ROWS, drain_a, 0)

        @pl.when(passes_on)
        def _():
            def drain(x, carry):
                c_copy(x).wait_send()
                return carry

            lax.fori_loop(lo_b, hi_b + 1, drain, 0)


def shards(
    starts, zone_map, zone_velocity, conductivity, x_velocity, cross_velocity, coarse_kernel
):
    smem = pl.BlockSpec(memory_space=pltpu.SMEM)
    vmem = pl.BlockSpec(memory_space=pltpu.VMEM)
    field = lambda rows: pltpu.VMEM((rows, NZ, NY), jnp.float32)
    dma = pltpu.SemaphoreType.DMA
    return pl.pallas_call(
        kernel,
        name="parareal",
        out_shape=jax.ShapeDtypeStruct(starts.shape, jnp.float32),
        in_specs=[smem] * 5 + [vmem] * 2,
        out_specs=vmem,
        scratch_shapes=[
            pltpu.VMEM((NY, NY), jnp.float32),
            pltpu.VMEM((2, WIDE, NZ, NY), jnp.float32),
            field(ROWS),
            field(EXT),
            pltpu.VMEM((7, WIDE, NZ, NY), jnp.float32),
            field(ROWS),
            field(EXT),
            field(EXT),
            field(EXT),
            field(EXT),
            field(EXT),
            field(ROWS),
            field(5),
            dma((2, 2)),
            dma((2, 2)),
            dma((2,)),
            dma((2,)),
            dma((2,)),
            dma((2,)),
            dma,
            dma((6,)),
            dma((2,)),
            dma((2,)),
            dma((2, ROWS)),
            dma((EXT,)),
            dma((2, ROWS)),
            dma((EXT,)),
            dma,
            dma,
            dma((EXT,)),
            dma((EXT,)),
            dma((ROWS,)),
            dma((ROWS,)),
        ],
        compiler_params=pltpu.CompilerParams(
            collective_id=0, has_side_effects=True, vmem_limit_bytes=56 * 2**20
        ),
    )(
        zone_velocity, conductivity, x_velocity, cross_velocity, coarse_kernel, starts, zone_map
    )


def solution(mesh):
    in_specs = (P("tm", "space", None, None), P("space", None, None), P(), P(), P(), P(), P())
    out_specs = P("tm", "space", None, None)
    return jax.shard_map(shards, mesh=mesh, in_specs=in_specs, out_specs=out_specs, check_vma=False)
```

time: 189 us -> 113 us (0.60)
  Pallas kernels: 187 us -> 110 us
    pallas_call x1, Pallas kernels: 187 us -> 110 us  [shards(): pl.pallas_call(kernel, name='parareal', out_shape=jax.ShapeDtypeStruct(st...]
where the time goes in v2:
time: 113 us; the launch traced here: 112 us
  Pallas kernels  110 us (97%)
  local copies, waits for them, and re-layouts  1.88 us (2%)
    pallas_call x1, Pallas kernels, shards(): pl.pallas_call(kernel, name='parareal', out_shape=jax.ShapeDtypeStruct(st...  110 us

profile of v2, /device:TPU:481, one launch (start us, length us, event | category | flops | bytes accessed | tf_op | source)
XLA Modules:
  0.0 112.3 jit_solution(1688139537300586528)
XLA Ops:
  0.0 110.4 %parareal.1 = f32[1,16,16,512]{3,2,1,0:T(8,128)} custom-call(s32[16]{0:T(128)} %zv.1, f32[16]{0:T(128)} %cond.1, f32[16]{0:T(128)} %xv.1, f32[2,16]{1,0:T(2,128)} %cv.1, f32[3,3,3]{2,1,0:T(4,128)} %ck.1, f32[1,16,16,512]{3,2,1,0:T(8,128)} %starts.1, s32[16,16,512]{2,1,0:T(8,128)} %zmap.1), custom_call_target="tpu_custom_call" | custom-call | tf_op jit(solution)/shard_map/parareal/pallas_call | solution.py:722
  110.4 1.9 %copy.9 = f32[1,16,16,512]{3,2,1,0:T(8,128)} copy(f32[1,16,16,512]{3,2,1,0:T(8,128)} %parareal.1) | data formatting | bytes 1048576

commit v3 on v2

--- a/solution.py
+++ b/solution.py
@@ -16,6 +16,7 @@
 LANES = 128
 EXT = ROWS + 2 * FINE
 BLOCK = 8
+PIECE = 2
 PAD = 24
 WIDE = ROWS + 2 * PAD
 MESH = pl.DeviceIdType.MESH
@@ -86,11 +87,13 @@
     )
     next_t = jnp.where(chip < chips // 2, t + 2, t - 2)
     last_t = jnp.where(chip < chips // 2, t - 2, t + 2)
-    low_helper = [s == half - 5, s == half - 13]
-    high_helper = [s == half + 4, s == half + 12]
-    helps_up = jnp.logical_or(low_helper[0], low_helper[1])
-    helps_down = jnp.logical_or(high_helper[0], high_helper[1])
-    helps = jnp.logical_or(helps_up, helps_down)
+    helpers = ((half - 4, half - 13, half - 12, half - 15), (half + 3, half + 12, half + 11, half + 14))
+
+    def any_of(flags):
+        return functools.reduce(jnp.logical_or, flags)
+
+    helps_up = any_of([s == h for h in helpers[0]])
+    helps_down = any_of([s == h for h in helpers[1]])
 
     def at(tm, space):
         return {"tm": tm, "space": space}
@@ -115,9 +118,6 @@
 
     @pl.when(far)
     def _():
-        greet(t, jnp.where(far_low, half - 5, half + 4))
-        greet(t, jnp.where(far_low, half - 13, half + 12))
-
         @pl.when(end_chip)
         def _():
             greet(across, over)
@@ -126,7 +126,7 @@
         def _():
             greet(last_t, s)
 
-    @pl.when(helps)
+    @pl.when(jnp.logical_or(helps_up, helps_down))
     def _():
         greet(t, jnp.where(helps_up, half - 1, half))
 
@@ -201,21 +201,20 @@
         + count(both(odd, t < slices - 1))
         + count(seeds)
         + count(goes_on)
-        + 2 * count(far)
-        + count(helps),
+        + len(helpers[0]) * count(far),
     )
 
     def z_half(side, c):
         at_row = FINE - BLOCK - BLOCK * c if side == 0 else FINE + ROWS + BLOCK * c
         return zone.at[pl.ds(at_row, BLOCK)]
 
-    def z_copy(side, tm, space):
+    def z_copy(side, tm, space, part):
         source = FINE + BLOCK - BLOCK * core if side == 0 else FINE + BLOCK * core
         return remote(
-            zone.at[pl.ds(source, BLOCK)],
-            z_half(side, core),
-            z_send.at[side],
-            z_recv.at[side],
+            zone.at[pl.ds(source + PIECE * part, PIECE)],
+            z_half(side, core).at[pl.ds(PIECE * part, PIECE)],
+            z_send.at[side, part],
+            z_recv.at[side, part],
             at(tm, space),
         )
 
@@ -228,26 +227,30 @@
         part = z_half(side, 1 - core)
         remote(part, part, zm_send.at[side], zm_recv.at[side], at(mate, s)).wait_recv()
 
-    def z_next(side):
-        part = z_half(side, core)
-        return remote(part, part, zf_send, z_recv.at[side], at(next_t, s))
+    def z_next(side, part):
+        rows = z_half(side, core).at[pl.ds(PIECE * part, PIECE)]
+        return remote(rows, rows, zf_send.at[part], z_recv.at[side, part], at(next_t, s))
 
     def each_zone_copy(act):
+        @pl.when(both(far_high, end_chip))
+        def _():
+            for part in range(BLOCK // PIECE):
+                act(z_copy(0, across, s + 1, part))
+
+        @pl.when(both(far_low, end_chip))
+        def _():
+            for part in range(BLOCK // PIECE):
+                act(z_copy(1, across, s - 1, part))
+
         @pl.when(both(has_high, jnp.logical_not(far_high)))
         def _():
-            act(z_copy(0, t, s + 1))
+            for part in range(BLOCK // PIECE):
+                act(z_copy(0, t, s + 1, part))
 
         @pl.when(both(has_low, jnp.logical_not(far_low)))
         def _():
-            act(z_copy(1, t, s - 1))
-
-        @pl.when(both(far_high, end_chip))
-        def _():
-            act(z_copy(0, across, s + 1))
-
-        @pl.when(both(far_low, end_chip))
-        def _():
-            act(z_copy(1, across, s - 1))
+            for part in range(BLOCK // PIECE):
+                act(z_copy(1, t, s - 1, part))
 
     def u_rows(start_row, rows):
         return u.at[0, pl.ds(PAD + start_row, rows)]
@@ -265,7 +268,18 @@
             at(t, space),
         )
 
-    pieces = ((0, 0, 4, -1), (0, 4, 2, 0), (0, 6, 2, 1), (1, 8, 2, -1), (1, 10, 3, 0), (1, 13, 3, 1))
+    pieces = (
+        (0, 2, 2, 0),
+        (0, 4, 1, 1),
+        (0, 5, 2, 2),
+        (0, 7, 1, 3),
+        (0, 0, 2, -1),
+        (1, 9, 2, 0),
+        (1, 11, 2, 1),
+        (1, 13, 1, 2),
+        (1, 14, 2, 3),
+        (1, 8, 1, -1),
+    )
 
     def piece_copy(side, number):
         batch, skip, rows, helper = pieces[number]
@@ -275,9 +289,7 @@
             dst, recv, space = u_rows(to, rows), u_recv.at[side, batch], half if side == 0 else half - 1
         else:
             dst, recv = rbuf.at[pl.ds(2 * batch, rows)], r_recv.at[batch]
-            space = (
-                (half - 5, half - 13)[helper] if side == 0 else (half + 4, half + 12)[helper]
-            )
+            space = helpers[side][helper]
         return remote(first.at[pl.ds(source, rows)], dst, r_send.at[number], recv, at(t, space))
 
     def forward_copy(side, number):
@@ -296,18 +308,17 @@
 
             @pl.when(flag)
             def _():
-                for number in (1, 2, 0, 4, 5, 3):
+                for number in range(len(pieces)):
                     act(piece_copy(side, number))
 
-    def each_forward(act):
-        for side, flags in ((0, low_helper), (1, high_helper)):
-            for helper in range(2):
-
-                @pl.when(flags[helper])
-                def _():
-                    for number in range(len(pieces)):
-                        if pieces[number][3] == helper:
-                            act(side, number)
+    def each_forward(side, act):
+        for helper, space in enumerate(helpers[side]):
+
+            @pl.when(s == space)
+            def _():
+                for number in range(len(pieces)):
+                    if pieces[number][3] == helper:
+                        act(side, number)
 
     def each_state_copy(batch, act):
         @pl.when(both(has_high, jnp.logical_not(far_high)))
@@ -381,25 +392,43 @@
         piece_copy(side, number).wait_recv()
         forward_copy(side, number).start()
 
-    each_forward(forward)
-
-    for side, flag, is_far in ((0, has_low, far_low), (1, has_high, far_high)):
-
-        @pl.when(flag)
-        def _():
-            z_copy(side, t, s).wait_recv()
-            z_mate(side).start()
-
-            @pl.when(both(is_far, goes_on))
+    each_forward(1, forward)
+
+    sides = ((0, has_low, far_low), (1, has_high, far_high))
+
+    def take_zones(side, hand_on):
+        for part in range(BLOCK // PIECE):
+            z_copy(side, t, s, part).wait_recv()
+
+            @pl.when(hand_on)
             def _():
-                z_next(side).start()
-
-    for side, flag in ((0, has_low), (1, has_high)):
-
-        @pl.when(flag)
-        def _():
-            z_mate_wait(side)
-            lax.fori_loop(-FINE if side == 0 else ROWS, 0 if side == 0 else ROWS + FINE, weights, 0)
+                z_next(side, part).start()
+
+        z_mate(side).start()
+
+    def side_weights(side):
+        z_mate_wait(side)
+        lax.fori_loop(-FINE if side == 0 else ROWS, 0 if side == 0 else ROWS + FINE, weights, 0)
+
+    for side, flag, is_far in sides:
+
+        @pl.when(both(flag, jnp.logical_not(is_far)))
+        def _():
+            take_zones(side, False)
+
+    for side, flag, is_far in sides:
+
+        @pl.when(both(flag, jnp.logical_not(is_far)))
+        def _():
+            side_weights(side)
+
+    for side, flag, is_far in sides:
+
+        @pl.when(both(is_far, goes_on))
+        def _():
+            take_zones(side, True)
+
+    each_forward(0, forward)
 
     def state_wait(side, batch):
         u_copy(side, batch).wait_recv()
@@ -463,6 +492,16 @@
 
         lax.fori_loop(0, FINE // 2, pair, 0)
 
+    for side, flag, is_far in sides:
+
+        @pl.when(both(is_far, jnp.logical_not(goes_on)))
+        def _():
+            take_zones(side, False)
+
+        @pl.when(is_far)
+        def _():
+            side_weights(side)
+
     @pl.when(ascending)
     def _():
         state_wait(1, 0)
@@ -678,8 +717,9 @@
     each_piece(sent)
     each_state_copy(0, sent)
     each_state_copy(1, sent)
-    each_forward(lambda side, number: forward_copy(side, number).wait_send())
-    for side, flag, is_far in ((0, has_low, far_low), (1, has_high, far_high)):
+    for side in range(2):
+        each_forward(side, lambda side, number: forward_copy(side, number).wait_send())
+    for side, flag, is_far in sides:
 
         @pl.when(flag)
         def _():
@@ -687,7 +727,8 @@
 
             @pl.when(both(is_far, goes_on))
             def _():
-                z_next(side).wait_send()
+                for part in range(BLOCK // PIECE):
+                    z_next(side, part).wait_send()
 
     each_jump_copy(sent)
 
@@ -738,15 +779,15 @@
             field(EXT),
             field(EXT),
             field(ROWS),
-            field(5),
+            field(4),
             dma((2, 2)),
             dma((2, 2)),
+            dma((2, BLOCK // PIECE)),
+            dma((2, BLOCK // PIECE)),
             dma((2,)),
             dma((2,)),
-            dma((2,)),
-            dma((2,)),
-            dma,
-            dma((6,)),
+            dma((BLOCK // PIECE,)),
+            dma((10,)),
             dma((2,)),
             dma((2,)),
             dma((2, ROWS)),

time: 113 us -> 94.1 us (0.83)
  Pallas kernels: 110 us -> 92.1 us
    pallas_call x1, Pallas kernels: 110 us -> 92.1 us  [shards(): pl.pallas_call(kernel, name='parareal', out_shape=jax.ShapeDtypeStruct(st...]
where the time goes in v3:
time: 94.1 us; the launch traced here: 94 us
  Pallas kernels  92.1 us (98%)
  local copies, waits for them, and re-layouts  1.88 us (2%)
    pallas_call x1, Pallas kernels, shards(): pl.pallas_call(kernel, name='parareal', out_shape=jax.ShapeDtypeStruct(st...  92.1 us

profile of v3, /device:TPU:481, one launch (start us, length us, event | category | flops | bytes accessed | tf_op | source)
XLA Modules:
  0.0 94.0 jit_solution(7741651551778956780)
XLA Ops:
  0.0 92.1 %parareal.1 = f32[1,16,16,512]{3,2,1,0:T(8,128)} custom-call(s32[16]{0:T(128)} %zv.1, f32[16]{0:T(128)} %cond.1, f32[16]{0:T(128)} %xv.1, f32[2,16]{1,0:T(2,128)} %cv.1, f32[3,3,3]{2,1,0:T(4,128)} %ck.1, f32[1,16,16,512]{3,2,1,0:T(8,128)} %starts.1, s32[16,16,512]{2,1,0:T(8,128)} %zmap.1), custom_call_target="tpu_custom_call" | custom-call | tf_op jit(solution)/shard_map/parareal/pallas_call | solution.py:763
  92.1 1.9 %copy.9 = f32[1,16,16,512]{3,2,1,0:T(8,128)} copy(f32[1,16,16,512]{3,2,1,0:T(8,128)} %parareal.1) | data formatting | bytes 1048576

commit v4 on v3

--- a/solution.py
+++ b/solution.py
@@ -87,7 +87,14 @@
     )
     next_t = jnp.where(chip < chips // 2, t + 2, t - 2)
     last_t = jnp.where(chip < chips // 2, t - 2, t + 2)
-    helpers = ((half - 4, half - 13, half - 12, half - 15), (half + 3, half + 12, half + 11, half + 14))
+    columns = (half - 4, half - 16, half - 8, half - 13, half - 5)
+    helpers = (columns, tuple(parts - 1 - h for h in columns))
+
+    own_column = sum(
+        jnp.where(chip == n, h, 0) for n, h in enumerate((half - 12, half - 4, half - 8, half - 15))
+    )
+    jump_helper = (own_column, parts - 1 - own_column)
+    by_column = chip < 4
 
     def any_of(flags):
         return functools.reduce(jnp.logical_or, flags)
@@ -145,6 +152,12 @@
     @pl.when(both(odd, has_high))
     def _():
         greet(t - 1, s + 1)
+
+    for side in range(2):
+
+        @pl.when(both(both(even, by_column), s == jump_helper[side]))
+        def _():
+            greet(t + 1, half - 1 if side == 0 else half)
 
     greet(mate, s)
 
@@ -201,7 +214,8 @@
         + count(both(odd, t < slices - 1))
         + count(seeds)
         + count(goes_on)
-        + len(helpers[0]) * count(far),
+        + len(helpers[0]) * count(far)
+        + count(both(far, both(odd, by_column))),
     )
 
     def z_half(side, c):
@@ -270,14 +284,15 @@
 
     pieces = (
         (0, 2, 2, 0),
+        (0, 5, 2, 2),
         (0, 4, 1, 1),
-        (0, 5, 2, 2),
         (0, 7, 1, 3),
         (0, 0, 2, -1),
         (1, 9, 2, 0),
+        (1, 13, 1, 2),
         (1, 11, 2, 1),
-        (1, 13, 1, 2),
-        (1, 14, 2, 3),
+        (1, 15, 1, 4),
+        (1, 14, 1, 3),
         (1, 8, 1, -1),
     )
 
@@ -331,8 +346,8 @@
 
     start = lambda copy: copy.start()
     sent = lambda copy: copy.wait_send()
+    each_piece(start)
     each_zone_copy(start)
-    each_piece(start)
     each_state_copy(0, start)
     each_state_copy(1, start)
 
@@ -553,13 +568,37 @@
         buf = ja if on_even else jb
         send, recv = (ja_send, ja_recv) if on_even else (jb_send, jb_recv)
         to = FINE + (x - ROWS if up else x + ROWS)
+        if on_even:
+            device = at(t + 1, s + 1 if up else s - 1)
+        else:
+            crosses = both(far_high if up else far_low, by_column)
+            device = at(
+                jnp.where(crosses, t - 1, t),
+                jnp.where(crosses, jump_helper[0 if up else 1], s + 1 if up else s - 1),
+            )
+        return remote(buf.at[FINE + x], buf.at[to], send.at[1 if up else 0, x], recv.at[to], device)
+
+    def jump_relay(n, up):
+        x = ROWS - 1 - n if up else n
+        to = FINE + (x - ROWS if up else x + ROWS)
         return remote(
-            buf.at[FINE + x],
-            buf.at[to],
-            send.at[1 if up else 0, x],
-            recv.at[to],
-            at(t + 1 if on_even else t, s + 1 if up else s - 1),
+            jb.at[to],
+            jb.at[to],
+            jb_send.at[1 if up else 0, x],
+            jb_recv.at[to],
+            at(t + 1, half if up else half - 1),
         )
+
+    def each_jump_relay(act):
+        for up in (True, False):
+
+            @pl.when(both(both(even, by_column), s == jump_helper[0 if up else 1]))
+            def _():
+                def row(n, carry):
+                    act(jump_relay(n, up))
+                    return carry
+
+                lax.fori_loop(0, depth - 1, row, 0)
 
     def each_jump_copy(act):
         for on_even, flag, rows in ((True, even, depth), (False, odd, depth - 1)):
@@ -584,6 +623,12 @@
         j_mate().start()
 
     each_jump_copy(start)
+
+    def relay_jump(copy):
+        copy.wait_recv()
+        copy.start()
+
+    each_jump_relay(relay_jump)
 
     low_end = jnp.where(has_low, -FINE, 0)
     high_end = jnp.where(has_high, ROWS + FINE - 1, ROWS - 1)
@@ -731,6 +776,7 @@
                     z_next(side, part).wait_send()
 
     each_jump_copy(sent)
+    each_jump_relay(sent)
 
     @pl.when(even)
     def _():
@@ -787,7 +833,7 @@
             dma((2,)),
             dma((2,)),
             dma((BLOCK // PIECE,)),
-            dma((10,)),
+            dma((11,)),
             dma((2,)),
             dma((2,)),
             dma((2, ROWS)),

time: 94.1 us -> 89.5 us (0.951)
  Pallas kernels: 92.1 us -> 87.4 us
    pallas_call x1, Pallas kernels: 92.1 us -> 87.4 us  [shards(): pl.pallas_call(kernel, name='parareal', out_shape=jax.ShapeDtypeStruct(st...]
where the time goes in v4:
time: 89.5 us; the launch traced here: 89.3 us
  Pallas kernels  87.4 us (98%)
  local copies, waits for them, and re-layouts  1.88 us (2%)
    pallas_call x1, Pallas kernels, shards(): pl.pallas_call(kernel, name='parareal', out_shape=jax.ShapeDtypeStruct(st...  87.4 us
    unnamed x1, local copies, waits for them, and re-layouts  1.88 us

profile of v4, /device:TPU:481, one launch (start us, length us, event | category | flops | bytes accessed | tf_op | source)
XLA Modules:
  0.0 89.3 jit_solution(14623208098878547351)
XLA Ops:
  0.0 87.4 %parareal.1 = f32[1,16,16,512]{3,2,1,0:T(8,128)} custom-call(s32[16]{0:T(128)} %zv.1, f32[16]{0:T(128)} %cond.1, f32[16]{0:T(128)} %xv.1, f32[2,16]{1,0:T(2,128)} %cv.1, f32[3,3,3]{2,1,0:T(4,128)} %ck.1, f32[1,16,16,512]{3,2,1,0:T(8,128)} %starts.1, s32[16,16,512]{2,1,0:T(8,128)} %zmap.1), custom_call_target="tpu_custom_call" | custom-call | tf_op jit(solution)/shard_map/parareal/pallas_call | solution.py:809
  87.4 1.9 %copy.9 = f32[1,16,16,512]{3,2,1,0:T(8,128)} copy(f32[1,16,16,512]{3,2,1,0:T(8,128)} %parareal.1) | data formatting | bytes 1048576

commit v5 on v4

--- a/solution.py
+++ b/solution.py
@@ -87,11 +87,11 @@
     )
     next_t = jnp.where(chip < chips // 2, t + 2, t - 2)
     last_t = jnp.where(chip < chips // 2, t - 2, t + 2)
-    columns = (half - 4, half - 16, half - 8, half - 13, half - 5)
+    columns = (half - 4, half - 13, half - 12, half - 15)
     helpers = (columns, tuple(parts - 1 - h for h in columns))
 
     own_column = sum(
-        jnp.where(chip == n, h, 0) for n, h in enumerate((half - 12, half - 4, half - 8, half - 15))
+        jnp.where(chip == n, h, 0) for n, h in enumerate((half - 8, half - 5, half - 6, half - 7))
     )
     jump_helper = (own_column, parts - 1 - own_column)
     by_column = chip < 4
@@ -284,15 +284,14 @@
 
     pieces = (
         (0, 2, 2, 0),
+        (0, 4, 1, 1),
         (0, 5, 2, 2),
-        (0, 4, 1, 1),
         (0, 7, 1, 3),
         (0, 0, 2, -1),
         (1, 9, 2, 0),
+        (1, 11, 2, 1),
         (1, 13, 1, 2),
-        (1, 11, 2, 1),
-        (1, 15, 1, 4),
-        (1, 14, 1, 3),
+        (1, 14, 2, 3),
         (1, 8, 1, -1),
     )
 
@@ -448,15 +447,16 @@
     def state_wait(side, batch):
         u_copy(side, batch).wait_recv()
 
-    @pl.when(both(ascending, has_low))
-    def _():
-        state_wait(0, 0)
-        state_wait(0, 1)
-
-    @pl.when(both(jnp.logical_not(ascending), has_high))
-    def _():
-        state_wait(1, 0)
-        state_wait(1, 1)
+    def early(batch):
+        @pl.when(both(ascending, has_low))
+        def _():
+            state_wait(0, batch)
+
+        @pl.when(both(jnp.logical_not(ascending), has_high))
+        def _():
+            state_wait(1, batch)
+
+    early(0)
 
     @pl.when(ascending)
     def _():
@@ -466,13 +466,13 @@
     def _():
         start_coarse(ROWS - 1)
 
-    def block(src, dst, x0):
-        base = PAD + jnp.where(ascending, x0, ROWS - BLOCK - x0)
+    def block(src, dst, x0, count=BLOCK):
+        base = PAD + jnp.where(ascending, x0, ROWS - count - x0)
         rows = [
             [src[base + r - 1, :, j * LANES : (j + 1) * LANES] for j in range(TILES)]
-            for r in range(BLOCK + 2)
+            for r in range(count + 2)
         ]
-        for r in range(BLOCK):
+        for r in range(count):
             x = base + r
             v = rows[r + 1]
             low = [pltpu.roll(v[TILES - 1], 1, 1)] + v[:-1]
@@ -487,14 +487,21 @@
                 )
                 dst[x, :, sl] = (centre + along_x) + (along_y + along_z)
 
+    for level in range(1, ROWS - BLOCK // 2):
+        src, dst = u.at[(level + 1) % 2], u.at[level % 2]
+
+        def two_rows(m, carry):
+            block(src, dst, level - BLOCK + 2 * m, 2)
+            return carry
+
+        pairs = BLOCK + 4 - level
+        lax.fori_loop(0, pairs, two_rows, 0, unroll=3 if pairs % 3 == 0 else (2 if pairs % 2 == 0 else 1))
+
+    early(1)
+
     def wedge(n, carry):
         for src, dst, level in ((u.at[0], u.at[1], 2 * n + 1), (u.at[1], u.at[0], 2 * n + 2)):
-
-            def blocks(m, c):
-                block(src, dst, ROWS - level - BLOCK * m)
-                return c
-
-            lax.fori_loop(1, (2 * (FINE - level) + 7) // BLOCK + 1, blocks, 0)
+            block(src, dst, jnp.minimum(level - FINE, BLOCK - level))
         return carry
 
     lax.fori_loop(0, FINE // 2, wedge, 0)
@@ -750,13 +757,7 @@
 
         lax.fori_loop(0, ROWS, wait_a, 0)
 
-    out[...] = lax.dot_general(
-        co[...].reshape(ROWS * NZ, NY),
-        perm[...],
-        (((1,), (1,)), ((), ())),
-        precision=HIGH,
-        preferred_element_type=jnp.float32,
-    ).reshape(1, ROWS, NZ, NY)
+    out[...] = co[...]
 
     each_zone_copy(sent)
     each_piece(sent)
@@ -799,6 +800,20 @@
             lax.fori_loop(lo_b, hi_b + 1, drain, 0)
 
 
+def in_order(ends, out):
+    pi, yi = iotas((NY, NY))
+    turn = jnp.where(yi == TILES * lax.rem(pi, LANES) + pi // LANES, 1.0, 0.0).astype(jnp.bfloat16)
+    rest = ends[...].reshape(ROWS * NZ, NY)
+    parts = []
+    for _ in range(3):
+        parts.append(rest.astype(jnp.bfloat16))
+        rest = rest - parts[-1].astype(jnp.float32)
+    low, mid, top = (
+        jnp.dot(part, turn, preferred_element_type=jnp.float32) for part in reversed(parts)
+    )
+    out[...] = ((low + mid) + top).reshape(1, ROWS, NZ, NY)
+
+
 def shards(
     starts, zone_map, zone_velocity, conductivity, x_velocity, cross_velocity, coarse_kernel
 ):
@@ -806,10 +821,10 @@
     vmem = pl.BlockSpec(memory_space=pltpu.VMEM)
     field = lambda rows: pltpu.VMEM((rows, NZ, NY), jnp.float32)
     dma = pltpu.SemaphoreType.DMA
-    return pl.pallas_call(
+    ends = pl.pallas_call(
         kernel,
         name="parareal",
-        out_shape=jax.ShapeDtypeStruct(starts.shape, jnp.float32),
+        out_shape=jax.ShapeDtypeStruct(starts.shape[1:], jnp.float32),
         in_specs=[smem] * 5 + [vmem] * 2,
         out_specs=vmem,
         scratch_shapes=[
@@ -833,7 +848,7 @@
             dma((2,)),
             dma((2,)),
             dma((BLOCK // PIECE,)),
-            dma((11,)),
+            dma((10,)),
             dma((2,)),
             dma((2,)),
             dma((2, ROWS)),
@@ -853,6 +868,14 @@
     )(
         zone_velocity, conductivity, x_velocity, cross_velocity, coarse_kernel, starts, zone_map
     )
+    return pl.pallas_call(
+        in_order,
+        name="in_order",
+        out_shape=jax.ShapeDtypeStruct(starts.shape, jnp.float32),
+        in_specs=[vmem],
+        out_specs=vmem,
+        compiler_params=pltpu.CompilerParams(vmem_limit_bytes=16 * 2**20),
+    )(ends)
 
 
 def solution(mesh):

time: 89.5 us -> 88.1 us (0.984)
    pallas_call x1, Pallas kernels: 87.4 us -> 85.4 us  [shards(): pl.pallas_call(kernel, name='parareal', out_shape=jax.ShapeDtypeStruct(st...]
    pallas_call x0 -> x1, Pallas kernels: none -> 1.42 us  [shards(): pl.pallas_call(in_order, name='in_order', out_shape=jax.ShapeDtypeStruct(...]
    unnamed x1 -> x2, local copies, waits for them, and re-layouts: 1.88 us -> 1.03 us
where the time goes in v5:
time: 88.1 us; the launch traced here: 87.9 us
  Pallas kernels  86.9 us (99%)
  local copies, waits for them, and re-layouts  1.03 us (1%)
    pallas_call x1, Pallas kernels, shards(): pl.pallas_call(kernel, name='parareal', out_shape=jax.ShapeDtypeStruct(st...  85.4 us

profile of v5, /device:TPU:481, one launch (start us, length us, event | category | flops | bytes accessed | tf_op | source)
XLA Modules:
  0.0 87.9 jit_solution(13807309566906466010)
XLA Ops:
  0.0 85.4 %parareal.1.ends = f32[16,16,512]{2,1,0:T(8,128)} custom-call(s32[16]{0:T(128)} %zv.1, f32[16]{0:T(128)} %cond.1, f32[16]{0:T(128)} %xv.1, f32[2,16]{1,0:T(2,128)} %cv.1, f32[3,3,3]{2,1,0:T(4,128)} %ck.1, f32[1,16,16,512]{3,2,1,0:T(8,128)} %starts.1, s32[16,16,512]{2,1,0:T(8,128)} %zmap.1), custom_call_target="tpu_custom_call" | custom-call | tf_op jit(solution)/shard_map/parareal/pallas_call | solution.py:824
  85.4 0.0 copy-start
  85.4 1.0 %copy-done = f32[16,16,512]{2,1,0:T(8,128)S(1)} copy-done((f32[16,16,512]{2,1,0:T(8,128)S(1)}, f32[16,16,512]{2,1,0:T(8,128)}, u32[]{:S(2)}) %copy-start) | copy-done | bytes 524312
  86.5 1.4 %in_order.1 = f32[1,16,16,512]{3,2,1,0:T(8,128)} custom-call(f32[16,16,512]{2,1,0:T(8,128)S(1)} %copy-done), custom_call_target="tpu_custom_call" | custom-call | tf_op jit(solution)/shard_map/in_order/pallas_call | solution.py:871
Async XLA Ops:
  85.4 1.0 %copy-start = (f32[16,16,512]{2,1,0:T(8,128)S(1)}, f32[16,16,512]{2,1,0:T(8,128)}, u32[]{:S(2)}) copy-start(f32[16,16,512]{2,1,0:T(8,128)} %parareal.1.ends) | copy-start | bytes 1572868
